TPU v7x, 32 devices: a whole 2x2x4 slice. The times are simulated.
32 devices in a mesh: dp: 8 (over y, x, core), tensor: 4 (over z).
Axes of the slice: x: 2, y: 2, z: 4, core: 2. Of those that a mesh axis runs over, the one named last changes fastest.
Arguments:
- tokens: bfloat16 [24, 577, 1024], P('dp', None, 'tensor'), may hold values from -6 to 6
- image_mask: int32 [24], P('dp'), may hold values 0 or 1
- ln1_gain: bfloat16 [1024], P('tensor'), may hold values from 0.5 to 1.5
- first_norm_bias: bfloat16 [1024], P('tensor'), may hold values from -3 to 3
- w_attn: bfloat16 [1024, 3, 1024], P(None, None, 'tensor'), may hold values from -0.1875 to 0.1875
- qv_bias: bfloat16 [2, 1024], P(None, 'tensor'), may hold values from -3 to 3
- w_out: bfloat16 [1024, 1024], P('tensor'), may hold values from -0.75 to 0.75
- b_out: bfloat16 [1024], P('tensor'), may hold values from -3 to 3
- ln2_gain: bfloat16 [1024], P('tensor'), may hold values from 0.5 to 1.5
- second_norm_bias: bfloat16 [1024], P('tensor'), may hold values from -3 to 3
- w_fc1: bfloat16 [1024, 4096], P(None, 'tensor'), may hold values from -0.1875 to 0.1875
- b_fc1: bfloat16 [4096], P('tensor'), may hold values from -3 to 3
- w_fc2: bfloat16 [4096, 1024], P('tensor'), may hold values from -0.09375 to 0.09375
- b_fc2: bfloat16 [1024], P('tensor'), may hold values from -3 to 3
- cotangent: bfloat16 [24, 577, 1024], P('dp', None, 'tensor'), may hold values from -6 to 6
Outputs:
- block_out: bfloat16 [24, 577, 1024], P('dp', None, 'tensor')
- input_grad: bfloat16 [24, 577, 1024], P('dp', None, 'tensor')
- first_norm_gain_gradient: float32 [1024], P('tensor')
- grad_ln1_bias: float32 [1024], P('tensor')
- grad_w_attn: float32 [1024, 3, 1024], P(None, None, 'tensor')
- grad_qv_bias: float32 [2, 1024], P(None, 'tensor')
- grad_w_out: float32 [1024, 1024], P('tensor')
- grad_b_out: float32 [1024], P('tensor')
- second_norm_gain_gradient: float32 [1024], P('tensor')
- grad_ln2_bias: float32 [1024], P('tensor')
- grad_w_fc1: float32 [1024, 4096], P(None, 'tensor')
- grad_b_fc1: float32 [4096], P('tensor')
- grad_w_fc2: float32 [4096, 1024], P('tensor')
- grad_b_fc2: float32 [1024], P('tensor')
All inputs are finite; a program needn't handle non-finite values. No bound on the sum of `image_mask` on one device may be relied on, other than what follows from the above.
Results may differ from a plain program's by a relative error of at most 0.014.
Values may be sent and summed in bfloat16 or wider, within the bound.
A program may use at most 128 MiB of HBM per device.

v0:
```python
import jax
import jax.numpy as jnp
from jax import lax
from jax.sharding import PartitionSpec as P

MODEL_WIDTH = 1024
HD = 64


EPS = 1e-05


def norm_stats(value):
    total, squares = lax.psum((jnp.sum(value, 1), jnp.sum(value * value, 1)), "tensor")
    middle = total / MODEL_WIDTH
    spread = squares / MODEL_WIDTH - middle * middle
    return (middle[:, None], lax.rsqrt(spread + EPS)[:, None])


def layer_norm_reverse(incoming_gradient, normalized_input, norm_gain, inverse_deviation):
    gain_scaled_gradient = incoming_gradient * norm_gain
    first_norm_result, second_norm_result = lax.psum(
        (jnp.sum(gain_scaled_gradient, 1), jnp.sum(gain_scaled_gradient * normalized_input, 1)),
        "tensor",
    )
    return inverse_deviation * (
        gain_scaled_gradient
        - first_norm_result[:, None] / MODEL_WIDTH
        - normalized_input * second_norm_result[:, None] / MODEL_WIDTH
    )


def spread_features(value):
    return lax.all_gather(value, "tensor", axis=1, tiled=True)


def settle_sums(value):
    return lax.psum_scatter(value, "tensor", scatter_dimension=1, tiled=True)


def pair_dot(left, right):
    return lax.dot_general(
        left, right, (((0,), (0,)), ((), ())), preferred_element_type=jnp.float32
    )


def back_dot(left, right):
    return lax.dot_general(
        left, right, (((1,), (1,)), ((), ())), preferred_element_type=jnp.float32
    )


def attend_image(blocks):
    query, keys, values = blocks
    scale = HD ** (-0.5)
    scores = jnp.einsum("qhd,khd->hqk", query, keys, preferred_element_type=jnp.float32) * scale
    top = jnp.max(scores, -1, keepdims=True)
    expo = jnp.exp(scores - top)
    total = jnp.sum(expo, -1, keepdims=True)
    probs = expo / total
    log_total = top[..., 0] + jnp.log(total[..., 0])
    context = jnp.einsum(
        "hqk,khd->qhd", probs.astype(jnp.bfloat16), values, preferred_element_type=jnp.float32
    )
    return (context.astype(jnp.bfloat16), log_total)


def attend_back(blocks):
    query, keys, values, log_total, dcontext = blocks
    scale = HD ** (-0.5)
    scores = jnp.einsum("qhd,khd->hqk", query, keys, preferred_element_type=jnp.float32) * scale
    probs = jnp.exp(scores - log_total[..., None])
    dvalues = jnp.einsum(
        "hqk,qhd->khd", probs.astype(jnp.bfloat16), dcontext, preferred_element_type=jnp.float32
    )
    dprobs = jnp.einsum("qhd,khd->hqk", dcontext, values, preferred_element_type=jnp.float32)
    delta = jnp.sum(probs * dprobs, -1, keepdims=True)
    dscores = (probs * (dprobs - delta)).astype(jnp.bfloat16)
    dquery = jnp.einsum("hqk,khd->qhd", dscores, keys, preferred_element_type=jnp.float32) * scale
    dkeys = jnp.einsum("hqk,qhd->khd", dscores, query, preferred_element_type=jnp.float32) * scale
    return jnp.stack([dquery, dkeys, dvalues], 1).astype(jnp.bfloat16)


def local(
    tokens,
    image_mask,
    ln1_gain,
    first_norm_bias,
    w_attn,
    qv_bias,
    w_out,
    b_out,
    ln2_gain,
    second_norm_bias,
    w_fc1,
    b_fc1,
    w_fc2,
    b_fc2,
    cotangent,
):
    images, seq, width_dev = tokens.shape
    rows = images * seq
    heads_dev = width_dev // HD
    mask_rows = jnp.repeat(image_mask.astype(jnp.float32), seq)[:, None]
    first_norm_gain = ln1_gain.astype(jnp.float32)
    second_norm_gain = ln2_gain.astype(jnp.float32)
    block_inputs = tokens.astype(jnp.float32).reshape(rows, width_dev)
    first_midpoint_state, first_inverse_deviation = norm_stats(block_inputs)
    first_normalized_input = (block_inputs - first_midpoint_state) * first_inverse_deviation
    h1_full = spread_features(
        (first_normalized_input * first_norm_gain + first_norm_bias.astype(jnp.float32)).astype(
            jnp.bfloat16
        )
    )
    qkv = jnp.einsum("nd,dce->nce", h1_full, w_attn, preferred_element_type=jnp.float32)
    bias_rows = qv_bias.astype(jnp.float32)
    bias_full = jnp.stack([bias_rows[0], jnp.zeros_like(bias_rows[0]), bias_rows[1]], 0)
    qkv = (qkv + bias_full).astype(jnp.bfloat16)
    query = qkv[:, 0].reshape(images, seq, heads_dev, HD)
    keys = qkv[:, 1].reshape(images, seq, heads_dev, HD)
    values = qkv[:, 2].reshape(images, seq, heads_dev, HD)
    context, log_total = lax.map(attend_image, (query, keys, values))
    context_flat = context.reshape(rows, width_dev)
    attn = settle_sums(
        jnp.dot(context_flat, w_out, preferred_element_type=jnp.float32)
    ) + b_out.astype(jnp.float32)
    residual_stream_state = block_inputs + attn
    second_midpoint_state, second_inverse_deviation = norm_stats(residual_stream_state)
    second_normalized_input = (
        residual_stream_state - second_midpoint_state
    ) * second_inverse_deviation
    h2_full = spread_features(
        (second_normalized_input * second_norm_gain + second_norm_bias.astype(jnp.float32)).astype(
            jnp.bfloat16
        )
    )
    hidden = jnp.dot(h2_full, w_fc1, preferred_element_type=jnp.float32) + b_fc1.astype(jnp.float32)
    sigma = jax.nn.sigmoid(1.702 * hidden)
    act = (hidden * sigma).astype(jnp.bfloat16)
    mlp = settle_sums(jnp.dot(act, w_fc2, preferred_element_type=jnp.float32)) + b_fc2.astype(
        jnp.float32
    )
    block_out = (
        ((residual_stream_state + mlp) * mask_rows)
        .astype(jnp.bfloat16)
        .reshape(images, seq, width_dev)
    )
    output_gradient = cotangent.astype(jnp.float32).reshape(rows, width_dev) * mask_rows
    dy_full = spread_features(output_gradient.astype(jnp.bfloat16))
    grad_b_fc2 = jnp.sum(output_gradient, 0)
    grad_w_fc2 = pair_dot(act, dy_full)
    dact = back_dot(dy_full, w_fc2)
    dhidden = (dact * (sigma + 1.702 * hidden * sigma * (1.0 - sigma))).astype(jnp.bfloat16)
    grad_b_fc1 = jnp.sum(dhidden, 0, dtype=jnp.float32)
    grad_w_fc1 = pair_dot(h2_full, dhidden)
    second_hidden_gradient = settle_sums(back_dot(dhidden, w_fc1))
    second_norm_gain_gradient = jnp.sum(second_hidden_gradient * second_normalized_input, 0)
    grad_ln2_bias = jnp.sum(second_hidden_gradient, 0)
    residual_gradient = output_gradient + layer_norm_reverse(
        second_hidden_gradient, second_normalized_input, second_norm_gain, second_inverse_deviation
    )
    dattn = residual_gradient.astype(jnp.bfloat16)
    grad_b_out = jnp.sum(dattn, 0, dtype=jnp.float32)
    dattn_full = spread_features(dattn)
    grad_w_out = pair_dot(context_flat, dattn_full)
    dcontext = back_dot(dattn_full, w_out).astype(jnp.bfloat16).reshape(images, seq, heads_dev, HD)
    dqkv = lax.map(attend_back, (query, keys, values, log_total, dcontext))
    dqkv = dqkv.reshape(rows, 3, width_dev)
    grad_w_attn = jnp.einsum("nd,nce->dce", h1_full, dqkv, preferred_element_type=jnp.float32)
    bias_sums = jnp.sum(dqkv, 0, dtype=jnp.float32)
    grad_qv_bias = jnp.stack([bias_sums[0], bias_sums[2]], 0)
    first_hidden_gradient = settle_sums(
        jnp.einsum("nce,dce->nd", dqkv, w_attn, preferred_element_type=jnp.float32)
    )
    first_norm_gain_gradient = jnp.sum(first_hidden_gradient * first_normalized_input, 0)
    grad_ln1_bias = jnp.sum(first_hidden_gradient, 0)
    input_grad = (
        (
            residual_gradient
            + layer_norm_reverse(
                first_hidden_gradient,
                first_normalized_input,
                first_norm_gain,
                first_inverse_deviation,
            )
        )
        .astype(jnp.bfloat16)
        .reshape(images, seq, width_dev)
    )
    (
        first_norm_gain_gradient,
        grad_ln1_bias,
        grad_w_attn,
        grad_qv_bias,
        grad_w_out,
        grad_b_out,
        second_norm_gain_gradient,
        grad_ln2_bias,
        grad_w_fc1,
        grad_b_fc1,
        grad_w_fc2,
        grad_b_fc2,
    ) = lax.psum(
        (
            first_norm_gain_gradient,
            grad_ln1_bias,
            grad_w_attn,
            grad_qv_bias,
            grad_w_out,
            grad_b_out,
            second_norm_gain_gradient,
            grad_ln2_bias,
            grad_w_fc1,
            grad_b_fc1,
            grad_w_fc2,
            grad_b_fc2,
        ),
        "dp",
    )
    return (
        block_out,
        input_grad,
        first_norm_gain_gradient,
        grad_ln1_bias,
        grad_w_attn,
        grad_qv_bias,
        grad_w_out,
        grad_b_out,
        second_norm_gain_gradient,
        grad_ln2_bias,
        grad_w_fc1,
        grad_b_fc1,
        grad_w_fc2,
        grad_b_fc2,
    )


def solution(mesh):
    in_specs = (
        P("dp", None, "tensor"),
        P("dp"),
        P("tensor"),
        P("tensor"),
        P(None, None, "tensor"),
        P(None, "tensor"),
        P("tensor", None),
        P("tensor"),
        P("tensor"),
        P("tensor"),
        P(None, "tensor"),
        P("tensor"),
        P("tensor", None),
        P("tensor"),
        P("dp", None, "tensor"),
    )
    out_specs = (
        P("dp", None, "tensor"),
        P("dp", None, "tensor"),
        P("tensor"),
        P("tensor"),
        P(None, None, "tensor"),
        P(None, "tensor"),
        P("tensor", None),
        P("tensor"),
        P("tensor"),
        P("tensor"),
        P(None, "tensor"),
        P("tensor"),
        P("tensor", None),
        P("tensor"),
    )
    return jax.shard_map(local, mesh=mesh, in_specs=in_specs, out_specs=out_specs, check_vma=False)
```

profile of v0, /device:TPU:0, one launch (start us, length us, event | category | flops | bytes accessed | tf_op | source)
XLA Modules:
  0.0 1169.9 jit_solution(11832118071449285978)
XLA Ops:
  12.0 20.5 %all-reduce.5 = (f32[1731]{0:T(1024)S(1)}, f32[1731]{0:T(1024)S(1)}) all-reduce(f32[1731]{0:T(1024)S(1)} %reduce_sum.169, f32[1731]{0:T(1024)S(1)} %reduce_sum.167), channel_id=1, replica_groups=mesh['dp'=8,'tensor'=4] {'tensor'}, use_global_device_ids=true, to_apply=%region_3.0 | all-reduce | flops 3462 | bytes 27696 | tf_op jit(solution)/shard_map/psum | solution.py:14
  32.5 2.9 add_convert_fusion.3
  35.7 68.3 %all-gather.5.cloned.1.call-done = bf16[1731,1024]{1,0:T(8,128)(2,1)} async-done(((bf16[1731,256]{1,0:T(8,128)(2,1)}), bf16[1731,1024]{1,0:T(8,128)(2,1)}) %all-gather.5.cloned.1.call-update) | async-done | bytes 3545104 | tf_op jit(solution)/shard_map/all_gather | solution.py:34
  103.9 5.4 add_convert_fusion
  113.5 3.0 copy.49
  116.4 3.9 reshape.158
  120.3 3.6 copy.48
  123.9 3.9 reshape.157
  127.9 3.6 copy.47
  131.4 19.0 %while.22 = (s32[]{:T(128)}, bf16[3,577,4,64]{1,3,2,0:T(8,128)(2,1)}, f32[3,4,577]{2,1,0:T(4,128)S(1)}, bf16[3,577,4,64]{1,3,2,0:T(8,128)(2,1)}, bf16[3,577,4,64...) while((s32[]{:T(128)}, bf16[3,577,4,64]{1,3,2,0:T(8,128)(2,1)}, ...), condition=%wide.region_7.8_spmd, body=%wide.region_4.7_spmd.sunk | while | flops 353050112 | bytes 17370328 | solution.py:122
  134.6 3.1 fusion.106
  140.9 3.1 fusion.106
  147.3 3.1 fusion.106
  150.4 3.1 copy.50
  153.5 3.7 reshape.148
  157.2 5.4 fusion.59
  163.2 121.7 %reduce-scatter.5.cloned.1.call-done = f32[1731,256]{1,0:T(8,128)} async-done(((f32[1731,1024]{1,0:T(8,128)}), f32[1731,256]{1,0:T(8,128)}) %reduce-scatter.5.cloned.1.call-update) | async-done | bytes 1772560 | tf_op jit(solution)/shard_map/reduce_scatter | solution.py:38
  285.0 3.4 fusion.55
  288.4 18.1 %all-reduce.4 = (f32[1731]{0:T(1024)S(1)}, f32[1731]{0:T(1024)S(1)}) all-reduce(f32[1731]{0:T(1024)S(1)} %get-tuple-element.122, f32[1731]{0:T(1024)S(1)} %get-tuple-element.121), channel_id=1, replica_groups=mesh['dp'=8,'tensor'=4] {'tensor'}, use_global_device_ids=true, to_apply=%region_12.13 | all-reduce | flops 3462 | bytes 27696 | tf_op jit(solution)/shard_map/psum | solution.py:14
  306.5 2.9 add_convert_fusion.2
  315.6 62.6 %all-gather.7.cloned.1.call-done = bf16[1731,1024]{1,0:T(8,128)(2,1)} async-done(((bf16[1731,256]{1,0:T(8,128)(2,1)}), bf16[1731,1024]{1,0:T(8,128)(2,1)}) %all-gather.7.cloned.1.call-update) | async-done | bytes 3545104 | tf_op jit(solution)/shard_map/all_gather | solution.py:34
  378.1 9.8 multiply_convert_fusion.2
  387.9 60.5 %all-gather.9.cloned.1.call-done = bf16[1731,1024]{1,0:T(8,128)(2,1)} async-done(((bf16[1731,256]{1,0:T(8,128)(2,1)}), bf16[1731,1024]{1,0:T(8,128)(2,1)}) %all-gather.9.cloned.1.call-update) | async-done | bytes 3545104 | tf_op jit(solution)/shard_map/all_gather | solution.py:34
  448.4 10.9 convert_reduce_fusion
  461.3 6.0 fusion.61
  468.8 8.3 fusion.60
  477.8 111.8 %reduce-scatter.9.cloned.1.call-done = f32[1731,256]{1,0:T(8,128)} async-done(((f32[1731,1024]{1,0:T(8,128)}), f32[1731,256]{1,0:T(8,128)}) %reduce-scatter.9.cloned.1.call-update) | async-done | bytes 1772560 | tf_op jit(solution)/shard_map/reduce_scatter | solution.py:38
  589.6 2.8 multiply_reduce_fusion.4
  592.4 18.4 %all-reduce.3 = (f32[1731]{0:T(1024)S(1)}, f32[1731]{0:T(1024)S(1)}) all-reduce(f32[1731]{0:T(1024)S(1)} %get-tuple-element.114, f32[1731]{0:T(1024)S(1)} %get-tuple-element.118), channel_id=1, replica_groups=mesh['dp'=8,'tensor'=4] {'tensor'}, use_global_device_ids=true, to_apply=%region_18.19 | all-reduce | flops 3462 | bytes 27696 | tf_op jit(solution)/shard_map/psum | solution.py:22
  610.9 105.9 %reduce-scatter.7.cloned.1.call-done = f32[1731,256]{1,0:T(8,128)} async-done(((f32[1731,1024]{1,0:T(8,128)}), f32[1731,256]{1,0:T(8,128)}) %reduce-scatter.7.cloned.1.call-update) | async-done | bytes 1772560 | tf_op jit(solution)/shard_map/reduce_scatter | solution.py:38
  716.7 5.8 convert_reduce_fusion.2
  722.7 70.6 %all-gather.11.cloned.1.call-done = bf16[1731,1024]{1,0:T(8,128)(2,1)} async-done(((bf16[1731,256]{1,0:T(8,128)(2,1)}), bf16[1731,1024]{1,0:T(8,128)(2,1)}) %all-gather.11.cloned.1.call-update) | async-done | bytes 3545104 | tf_op jit(solution)/shard_map/all_gather | solution.py:34
  793.3 3.2 convolution_convert_fusion
  799.3 3.7 copy.54
  803.0 26.9 %while.23 = (s32[]{:T(128)}, bf16[3,577,3,4,64]{1,4,3,2,0:T(8,128)(2,1)}, bf16[3,577,4,64]{1,3,2,0:T(8,128)(2,1)S(1)}, bf16[3,577,4,64]{1,3,2,0:T(8,128)(2,1)S(1...) while((s32[]{:T(128)}, ...), condition=%wide.region_21.22_spmd, body=%wide.region_19.21_spmd.sunk | while | flops 871673856 | bytes 50574628 | solution.py:167
  830.0 6.3 copy.56
  836.2 6.8 reshape.152
  843.1 7.5 convolution_bitcast_fusion
  850.9 9.3 fusion.63
  860.2 5.7 fusion.64
  869.2 4.9 fusion.52
  880.7 92.3 %reduce-scatter.11.cloned.1.call-done = f32[1731,256]{1,0:T(8,128)} async-done(((f32[1731,1024]{1,0:T(8,128)}), f32[1731,256]{1,0:T(8,128)}) %reduce-scatter.11.cloned.1.call-update) | async-done | bytes 1772560 | tf_op jit(solution)/shard_map/reduce_scatter | solution.py:38
  973.0 2.8 multiply_reduce_fusion.5
  975.8 18.0 %all-reduce.2 = (f32[1731]{0:T(1024)S(1)}, f32[1731]{0:T(1024)S(1)}) all-reduce(f32[1731]{0:T(1024)S(1)} %get-tuple-element.116, f32[1731]{0:T(1024)S(1)} %get-tuple-element.117), channel_id=1, replica_groups=mesh['dp'=8,'tensor'=4] {'tensor'}, use_global_device_ids=true, to_apply=%region_26.27 | all-reduce | flops 3462 | bytes 27696 | tf_op jit(solution)/shard_map/psum | solution.py:22
  993.8 2.9 add_convert_fusion.1
  997.8 23.7 %all-reduce = (f32[256]{0:T(256)}, f32[256]{0:T(256)}, f32[2,256]{1,0:T(2,128)}, f32[256]{0:T(256)}, f32[256]{0:T(256)}, /*index=5*/f32[256]{0:T(256)}, f32[1024]{0:T(1024)}, f32[256]{0:T(256)}) all-reduce(f32[256]{0:T(256)S(1)} %get-tuple-element.115, f32[256]{0:T(256)S(1)} %get-tuple-element.120, ...), channel_id=1, replica_groups=mesh['dp'=8,'tensor'=4] {'dp'}, use_global_device_ids=true, to_apply=%region_28.29 | all-reduce | flops 3072 | bytes 24576 | tf_op jit(solution)/shard_map/psum | solution.py:203
  1021.5 131.0 %all-reduce.8.cloned.1.call-done = (f32[1024,3,256]{2,0,1:T(8,128)}, f32[256,1024]{1,0:T(8,128)}, f32[1024,1024]{1,0:T(8,128)}, f32[1024,1024]{1,0:T(8,128)}) async-done(((f32[1024,3,256]{2,0,1:T(8,128)}, f32[256,1024]{1,0:T(8,128)}, f32[1024,1024]{1,0:T(8,128)}, f32[1024,1024]{1,0:T(8,128)}), (f32[1024,3,256]{2,0,1:T(8,128)}, f32[256,1024]{1,0:T(8,128)}, f32[1024,1024]{1,0:T(8,128)}, ...) | async-done | bytes 12582928 | tf_op jit(solution)/shard_map/psum | solution.py:203
  1152.5 3.9 copy.97
  (168 shorter events, 77.1 us)
Async XLA Ops:
  7.2 370.9 %copy-start = (bf16[1024,1024]{1,0:T(8,128)(2,1)S(1)}, bf16[1024,1024]{1,0:T(8,128)(2,1)}, u32[]{:S(2)}) copy-start(bf16[1024,1024]{1,0:T(8,128)(2,1)} %param.29) | copy-start | bytes 6291460
  7.2 4.6 copy-start.27
  7.2 4.6 copy-start.28
  7.2 96.7 %all-gather.5.cloned.1.call-start = ((), (), s32[]{:S(2)}) async-start(), calls=%async_computation.4 | async-start | bytes 4444160 | tf_op jit(solution)/shard_map/all_gather | solution.py:34
  9.2 26.4 %copy-start.19 = (bf16[2,256]{1,0:T(2,128)(2,1)S(1)}, bf16[2,256]{1,0:T(2,128)(2,1)}, u32[]{:S(2)}) copy-start(bf16[2,256]{1,0:T(2,128)(2,1)} %param.24) | copy-start | bytes 3076
  11.8 92.1 %copy-start.17 = (f32[256]{0:T(256)}, f32[256]{0:T(256)S(1)}, u32[]{:S(2)}) copy-start(f32[256]{0:T(256)S(1)} %convert_element_type.97) | copy-start | bytes 3076
  32.5 71.5 %copy-start.13 = (f32[1731]{0:T(1024)}, f32[1731]{0:T(1024)S(1)}, u32[]{:S(2)}) copy-start(f32[1731]{0:T(1024)S(1)} %get-tuple-element.185) | copy-start | bytes 20776
  32.5 71.5 %copy-start.15 = (f32[1731]{0:T(1024)}, f32[1731]{0:T(1024)S(1)}, u32[]{:S(2)}) copy-start(f32[1731]{0:T(1024)S(1)} %get-tuple-element.186) | copy-start | bytes 20776
  35.4 249.5 %reduce-scatter.5.cloned.1.call-start = ((), (), s32[]{:S(2)}) async-start(), calls=%async_computation.5 | async-start | bytes 8888320 | tf_op jit(solution)/shard_map/reduce_scatter | solution.py:38
  162.6 0.7 copy-start.29
  162.6 0.7 copy-start.30
  162.6 0.7 copy-start.31
  162.6 215.5 %all-gather.7.cloned.1.call-start = ((), (), s32[]{:S(2)}) async-start(), calls=%async_computation.6 | async-start | bytes 4444160 | tf_op jit(solution)/shard_map/all_gather | solution.py:34
  288.4 21.1 %copy-start.32 = (s32[3]{0:T(128)S(1)}, s32[3]{0:T(128)}, u32[]{:S(2)}) copy-start(s32[3]{0:T(128)} %param.20) | copy-start | bytes 40
  309.4 139.0 %all-gather.9.cloned.1.call-start = ((), (), s32[]{:S(2)}) async-start(), calls=%async_computation.8 | async-start | bytes 4444160 | tf_op jit(solution)/shard_map/all_gather | solution.py:34
  309.5 0.5 copy-start.20
  310.2 5.4 copy-start.22
  315.5 274.1 %reduce-scatter.9.cloned.1.call-start = ((), (), s32[]{:S(2)}) async-start(), calls=%async_computation.9 | async-start | bytes 8888320 | tf_op jit(solution)/shard_map/reduce_scatter | solution.py:38
  459.4 1.9 copy-start.35
  467.2 1.6 copy-start.26
  467.2 249.5 %reduce-scatter.7.cloned.1.call-start = ((), (), s32[]{:S(2)}) async-start(), calls=%async_computation.7 | async-start | bytes 8888320 | tf_op jit(solution)/shard_map/reduce_scatter | solution.py:38
  477.2 0.7 copy-start.33
  477.2 112.5 %copy-start.4 = (f32[1731,256]{1,0:T(8,128)S(1)}, f32[1731,256]{1,0:T(8,128)}, u32[]{:S(2)}) copy-start(f32[1731,256]{1,0:T(8,128)} %get-tuple-element.174) | copy-start | bytes 5317636
  477.2 316.1 %all-gather.11.cloned.1.call-start = ((), (), s32[]{:S(2)}) async-start(), calls=%async_computation.10 | async-start | bytes 4444160 | tf_op jit(solution)/shard_map/all_gather | solution.py:34
  722.6 250.4 %reduce-scatter.11.cloned.1.call-start = ((), (), s32[]{:S(2)}) async-start(), calls=%async_computation.11 | async-start | bytes 8888320 | tf_op jit(solution)/shard_map/reduce_scatter | solution.py:38
  796.5 6.5 copy-start.3
  803.0 1.2 copy-start.5
  812.0 1.2 copy-start.5
  821.0 1.2 copy-start.5
  843.1 7.5 copy-start.10
  850.6 301.9 %all-reduce.8.cloned.1.call-start = ((), (), s32[]{:S(2)}) async-start(), calls=%async_computation.12 | async-start | bytes 25165824 | tf_op jit(solution)/shard_map/psum | solution.py:203
  850.8 9.3 copy-start.24
  850.9 9.3 copy-start.34
  860.1 5.7 copy-start.6
  860.2 5.7 copy-start.25
  865.9 2.2 copy-start.11
  865.9 3.3 copy-start.23
  874.1 1.2 copy-start.9
  874.1 1.2 copy-start.21
  875.2 97.7 %copy-start.2 = (f32[1731,256]{1,0:T(8,128)S(1)}, f32[1731,256]{1,0:T(8,128)}, u32[]{:S(2)}) copy-start(f32[1731,256]{1,0:T(8,128)} %reshape.147) | copy-start | bytes 5317636
  875.2 97.7 %copy-start.14 = (f32[1731]{0:T(1024)S(1)}, f32[1731]{0:T(1024)}, u32[]{:S(2)}) copy-start(f32[1731]{0:T(1024)} %copy-done.13) | copy-start | bytes 20776
  875.2 97.7 %copy-start.16 = (f32[1731]{0:T(1024)S(1)}, f32[1731]{0:T(1024)}, u32[]{:S(2)}) copy-start(f32[1731]{0:T(1024)} %copy-done.15) | copy-start | bytes 20776
  875.3 97.7 %copy-start.18 = (f32[256]{0:T(256)S(1)}, f32[256]{0:T(256)}, u32[]{:S(2)}) copy-start(f32[256]{0:T(256)} %copy-done.17) | copy-start | bytes 3076
  1152.5 3.9 copy-start.12
  1152.5 4.9 copy-start.8
  1157.4 3.7 copy-start.7
  1157.4 5.7 copy-start.1
Sparse Core Ops, SparseCore 0:
  35.6 68.3 all-gather.4
  162.7 122.2 reduce-scatter.4
  309.6 68.5 all-gather.6
  380.1 68.2 all-gather.8
  467.4 122.2 reduce-scatter.8
  591.8 124.8 reduce-scatter.6
  722.7 70.5 all-gather.10
  850.7 122.2 reduce-scatter.10
  978.1 174.3 all-reduce.7
where the time goes:
time: 1180 us; the launch traced here: 1170 us
  waiting for transfers between devices  825 us (70%)
  matrix products  114 us (10%)
  blocking collectives  98.8 us (8%)
  local copies, waits for them, and re-layouts  75.8 us (6%)
  other arithmetic  41.8 us (4%)
  between operations  14.4 us (1%)
    reduce_scatter x4, waiting for transfers between devices, settle_sums(): return lax.psum_scatter(value, 'tensor', scatter_dimension=1, tiled=True)  432 us
    all_gather x4, waiting for transfers between devices, spread_features(): return lax.all_gather(value, 'tensor', axis=1, tiled=True)  262 us
    psum x1, waiting for transfers between devices, local(): lax.psum((first_norm_gain_gradient, grad_ln1_bias, grad_w_attn, grad_qv_b...  131 us
    psum x2, blocking collectives, norm_stats(): lax.psum((jnp.sum(value, 1), jnp.sum(value * value, 1)), 'tensor')  38.6 us
    psum x2, blocking collectives, layer_norm_reverse(): lax.psum((jnp.sum(gain_scaled_gradient, 1), jnp.sum(gain_scaled_gradient...  36.4 us
    psum x1, blocking collectives, local(): lax.psum((first_norm_gain_gradient, grad_ln1_bias, grad_w_attn, grad_qv_b...  23.7 us
  transfers between devices with their start and end apart: 9, of which 9 were waited for; matrix products, arithmetic and copies ran while one was open for 5% of the time, Pallas kernels for 0%

commit v1 on v0

--- a/solution.py
+++ b/solution.py
@@ -1,6 +1,10 @@
+import functools
+
 import jax
 import jax.numpy as jnp
 from jax import lax
+from jax.experimental import pallas as pl
+from jax.experimental.pallas import tpu as pltpu
 from jax.sharding import PartitionSpec as P
 
 MODEL_WIDTH = 1024
@@ -235,6 +239,784 @@
     )
 
 
+RING = 4
+
+
+MESH_ID = pl.DeviceIdType.MESH
+PAD = 592
+
+
+def turned(p, q):
+    for bit in (1, 2, 4):
+        if q & bit:
+            p = p + bit - 2 * bit * lax.rem(p // bit, 2)
+    return p
+
+
+def greet(p, z):
+    barrier = pltpu.get_barrier_semaphore()
+    for d in range(1, RING):
+        pl.semaphore_signal(
+            barrier, inc=1, device_id=(p, lax.rem(z + d, RING)), device_id_type=MESH_ID
+        )
+    for q in (1, 2, 4, 6):
+        pl.semaphore_signal(barrier, inc=1, device_id=(turned(p, q), z), device_id_type=MESH_ID)
+    pl.semaphore_wait(barrier, 7)
+
+
+def gather_kernel(
+    images,
+    tokens,
+    cotangent,
+    small,
+    attn_in,
+    out_in,
+    fc1_in,
+    fc2_in,
+    x_full,
+    dy_full,
+    small_full,
+    attn_full,
+    out_full,
+    fc1_full,
+    fc2_full,
+    row_send,
+    row_recv,
+    small_send,
+    small_recv,
+    unit_send,
+    unit_recv,
+    local_sem,
+):
+    p = lax.axis_index("dp")
+    z = lax.axis_index("tensor")
+    core = lax.rem(p, 2)
+    width = tokens.shape[2]
+    greet(p, z)
+
+    def remote(src, dst, send, recv, target):
+        return pltpu.make_async_remote_copy(
+            src_ref=src,
+            dst_ref=dst,
+            send_sem=send,
+            recv_sem=recv,
+            device_id=target,
+            device_id_type=MESH_ID,
+        )
+
+    shifts = [lax.rem(z + d, RING) for d in range(RING)]
+
+    def holds(plane):
+        slot = plane - core
+        return (slot >= 0) & (slot < images)
+
+    def row_copy(which, source, target, d):
+        dest = shifts[d]
+        return remote(
+            source.at[jnp.clip(dest - core, 0, images - 1)],
+            target.at[:, pl.ds(pl.multiple_of(z * width, width), width)],
+            row_send.at[which, d],
+            row_recv.at[which, d],
+            (p, dest),
+        )
+
+    def row_start(which, source, target):
+        for d in range(1, RING):
+            pl.when(holds(shifts[d]))(row_copy(which, source, target, d).start)
+
+    def row_wait(which, source, target):
+        for d in range(1, RING):
+            pl.when(holds(shifts[d]))(row_copy(which, source, target, d).wait_send)
+            pl.when(holds(z))(row_copy(which, source, target, d).wait_recv)
+
+    def row_own(which, source, target):
+        return pltpu.make_async_copy(
+            source.at[jnp.clip(z - core, 0, images - 1)],
+            target.at[:, pl.ds(pl.multiple_of(z * width, width), width)],
+            local_sem.at[4, which],
+        )
+
+    def place(chunk, q, k):
+        if chunk == 0:
+            return attn_full.at[:, q // 2, k, q % 2]
+        if chunk == 1:
+            return out_full.at[q // 2, k, q % 2]
+        return (fc1_full if chunk == 2 else fc2_full).at[q, k]
+
+    pieces = (attn_in, out_in, fc1_in, fc2_in)
+
+    def own_copy(chunk, q):
+        return pltpu.make_async_copy(
+            pieces[chunk].at[turned(p, q)], place(chunk, q, 0), local_sem.at[chunk, q]
+        )
+
+    def z_copy(chunk, d):
+        return remote(
+            pieces[chunk].at[p],
+            place(chunk, 0, d),
+            unit_send.at[chunk, d, 0],
+            unit_recv.at[chunk, d, 0],
+            (p, shifts[d]),
+        )
+
+    def plane_copy(chunk, k, source, target):
+        flip = source ^ target
+        return remote(
+            place(chunk, source, k),
+            place(chunk, target, k),
+            unit_send.at[chunk, k, target],
+            unit_recv.at[chunk, k, target],
+            (turned(p, flip), z),
+        )
+
+    def small_copy(d):
+        return remote(small, small_full.at[d], small_send.at[d], small_recv.at[d], (p, shifts[d]))
+
+    small_own = pltpu.make_async_copy(small, small_full.at[0], local_sem.at[4, 2])
+
+    for d in range(1, RING):
+        small_copy(d).start()
+        z_copy(0, d).start()
+    row_start(0, tokens, x_full)
+    row_own(0, tokens, x_full).start()
+    small_own.start()
+    for chunk in range(4):
+        for q in range(8):
+            own_copy(chunk, q).start()
+    for d in range(1, RING):
+        z_copy(1, d).start()
+    for d in range(1, RING):
+        z_copy(2, d).start()
+    row_start(1, cotangent, dy_full)
+    row_own(1, cotangent, dy_full).start()
+    for d in range(1, RING):
+        z_copy(3, d).start()
+
+    def spread(chunk, k):
+        z_copy(chunk, k).wait_recv()
+        for target in (2, 4, 6, 1):
+            plane_copy(chunk, k, 0, target).start()
+
+    def share(chunk, k):
+        for q in (2, 4, 6):
+            plane_copy(chunk, k, 0, q).wait_recv()
+            plane_copy(chunk, k, q, q + 1).start()
+
+    for chunk in range(4):
+        for k in range(1, RING):
+            spread(chunk, k)
+        if chunk:
+            for k in range(1, RING):
+                share(chunk - 1, k)
+    for k in range(1, RING):
+        share(3, k)
+    for chunk in range(4):
+        for k in range(1, RING):
+            for target in (1, 3, 5, 7):
+                plane_copy(chunk, k, target - 1, target).wait_recv()
+    for chunk in range(4):
+        for q in range(8):
+            own_copy(chunk, q).wait()
+        for k in range(1, RING):
+            z_copy(chunk, k).wait_send()
+            for target in range(1, 8):
+                source = target - 1 if target % 2 else 0
+                plane_copy(chunk, k, source, target).wait_send()
+    for d in range(1, RING):
+        small_copy(d).wait()
+    small_own.wait()
+    row_wait(0, tokens, x_full)
+    row_wait(1, cotangent, dy_full)
+    row_own(0, tokens, x_full).wait()
+    row_own(1, cotangent, dy_full).wait()
+
+
+def gather_all(tokens, cotangent, small, attn_in, out_in, fc1_in, fc2_in):
+    images, rows, width = tokens.shape
+    full = RING * width
+    hid = fc1_in.shape[1]
+    bf16 = jnp.bfloat16
+    shapes = (
+        (rows, full),
+        (rows, full),
+        (RING,) + small.shape,
+        (3, 4, RING, 2, 32, full),
+        (4, RING, 2, 32, full),
+        (8, RING, hid, full),
+        (8, RING, hid, full),
+    )
+    dma = pltpu.SemaphoreType.DMA
+    return pl.pallas_call(
+        functools.partial(gather_kernel, images),
+        out_shape=[jax.ShapeDtypeStruct(s, bf16) for s in shapes],
+        in_specs=[pl.BlockSpec(memory_space=pl.ANY)] * 7,
+        out_specs=[pl.BlockSpec(memory_space=pl.ANY)] * 7,
+        scratch_shapes=[
+            dma((2, RING)),
+            dma((2, RING)),
+            dma((RING,)),
+            dma((RING,)),
+            dma((4, RING, 8)),
+            dma((4, RING, 8)),
+            dma((5, 8)),
+        ],
+        compiler_params=pltpu.CompilerParams(collective_id=0, has_side_effects=True),
+    )(tokens, cotangent, small, attn_in, out_in, fc1_in, fc2_in)
+
+
+def reduce_kernel(images, sizes, *refs):
+    (
+        block_in,
+        grad_in,
+        vector_in,
+        g2,
+        g1,
+        go,
+        ga,
+        block_out,
+        grad_out,
+        vector_out,
+        s2,
+        s1,
+        so,
+        sa,
+        held,
+        kept,
+        first,
+        second,
+        far,
+        total,
+        vec,
+        vec_far,
+        send,
+        recv,
+        row_send,
+        row_recv,
+        vec_send,
+        vec_recv,
+        local_sem,
+    ) = refs
+    p = lax.axis_index("dp")
+    z = lax.axis_index("tensor")
+    core = lax.rem(p, 2)
+    width = block_out.shape[2]
+    greet(p, z)
+    grads = (g2, g1, go, ga)
+    outs = (s2, s1, so, sa)
+    starts = [sum(sizes[:i]) for i in range(4)]
+
+    def remote(src, dst, ssem, rsem, target):
+        return pltpu.make_async_remote_copy(
+            src_ref=src,
+            dst_ref=dst,
+            send_sem=ssem,
+            recv_sem=rsem,
+            device_id=target,
+            device_id_type=MESH_ID,
+        )
+
+    def near(q):
+        return (turned(p, q), z)
+
+    shifts = [lax.rem(z + d, RING) for d in range(RING)]
+
+    slot = z - core
+    live = (slot >= 0) & (slot < images)
+
+    def columns(plane):
+        return pl.ds(pl.multiple_of(plane * width, width), width)
+
+    def row_copy(which, source, target, d):
+        return remote(
+            source.at[:, columns(shifts[d])],
+            target.at[jnp.clip(slot, 0, images - 1)],
+            row_send.at[which, d],
+            row_recv.at[which, d],
+            (p, shifts[d]),
+        )
+
+    def row_own(which, source, target):
+        return pltpu.make_async_copy(
+            source.at[:, columns(z)],
+            target.at[jnp.clip(slot, 0, images - 1)],
+            row_send.at[which, 0],
+        )
+
+    def row_start(which, source, target):
+        @pl.when(live)
+        def _():
+            row_own(which, source, target).start()
+            for d in range(1, RING):
+                row_copy(which, source, target, d).start()
+
+    def row_wait(which, source, target):
+        @pl.when(live)
+        def _():
+            row_own(which, source, target).wait()
+            for d in range(1, RING):
+                row_copy(which, source, target, d).wait_send()
+
+        for d in range(1, RING):
+            other = lax.rem(z + RING - d, RING) - core
+            pl.when((other >= 0) & (other < images))(
+                row_copy(which, source, target, d).wait_recv
+            )
+
+    def rows(chunk):
+        return pl.ds(starts[chunk], sizes[chunk])
+
+    def core_copy(c):
+        return remote(
+            grads[c].at[:, :, 1], held.at[:, :, :, rows(c)], send.at[c, 0], recv.at[c, 0], near(1)
+        )
+
+    def keep_copy(c):
+        return pltpu.make_async_copy(
+            grads[c].at[:, :, 0], kept.at[:, :, :, rows(c)], local_sem.at[c, 0]
+        )
+
+    def x_copy(c):
+        return remote(
+            held.at[:, 1, 0:2, rows(c)], first.at[0, :, :, rows(c)], send.at[c, 1], recv.at[c, 1], near(2)
+        )
+
+    def y_copy(c):
+        return remote(
+            held.at[1, :, 2:4, rows(c)], first.at[1, :, :, rows(c)], send.at[c, 2], recv.at[c, 2], near(4)
+        )
+
+    def xy_copy(c):
+        return remote(
+            first.at[0, 1, :, rows(c)], second.at[0, :, rows(c)], send.at[c, 3], recv.at[c, 3], near(4)
+        )
+
+    def yx_copy(c):
+        return remote(
+            first.at[1, 1, :, rows(c)], second.at[1, :, rows(c)], send.at[c, 4], recv.at[c, 4], near(2)
+        )
+
+    def z_copy(c, k):
+        return remote(
+            second.at[k // 2, k % 2, rows(c)],
+            far.at[k - 1, rows(c)],
+            send.at[c, 4 + k],
+            recv.at[c, 4 + k],
+            (p, shifts[RING - k]),
+        )
+
+    def out_copy(c, q):
+        return remote(
+            total.at[rows(c)], outs[c].at[p], send.at[c, 7 + q], recv.at[c, 7 + q], near(q)
+        )
+
+    def out_own(c):
+        return pltpu.make_async_copy(total.at[rows(c)], outs[c].at[p], local_sem.at[c, 1])
+
+    def share_copy(c, q):
+        return remote(
+            outs[c].at[turned(p, q)],
+            outs[c].at[turned(p, q)],
+            send.at[c, 8 + q],
+            recv.at[c, 8 + q],
+            near(1),
+        )
+
+    def share_wait(c, q):
+        return remote(
+            outs[c].at[turned(p, q)],
+            outs[c].at[turned(p, q + 1)],
+            send.at[c, 8 + q],
+            recv.at[c, 8 + q],
+            near(1),
+        )
+
+    step = 16
+
+    def add(dest, *sources):
+        def body(i, _):
+            at = pl.ds(pl.multiple_of(i * step, step), step)
+            value = sources[0][at].astype(jnp.float32)
+            for s in sources[1:]:
+                value = value + s[at].astype(jnp.float32)
+            dest[at] = value.astype(dest.dtype)
+            return 0
+
+        lax.fori_loop(0, dest.shape[0] // step, body, 0)
+
+    def merge(c, y, x, ks):
+        for k in ks:
+            block = held.at[y, x, k, rows(c)]
+            add(block, block, kept.at[y, x, k, rows(c)])
+
+    def stage(c, s):
+        if s == 0:
+            core_copy(c).start()
+            keep_copy(c).start()
+        elif s == 1:
+            core_copy(c).wait_recv()
+            keep_copy(c).wait()
+            for y in range(2):
+                merge(c, y, 1, (0, 1))
+            x_copy(c).start()
+            for x in range(2):
+                merge(c, 1, x, (2, 3))
+            y_copy(c).start()
+            for y in range(2):
+                merge(c, y, 0, (0, 1))
+            for x in range(2):
+                merge(c, 0, x, (2, 3))
+        elif s == 2:
+            x_copy(c).wait_recv()
+            for k in range(2):
+                block = first.at[0, 1, k, rows(c)]
+                add(block, block, held.at[1, 0, k, rows(c)])
+            xy_copy(c).start()
+            y_copy(c).wait_recv()
+            for k in range(2):
+                block = first.at[1, 1, k, rows(c)]
+                add(block, block, held.at[0, 1, 2 + k, rows(c)])
+            yx_copy(c).start()
+        elif s == 3:
+            xy_copy(c).wait_recv()
+            for k in range(2):
+                block = second.at[0, k, rows(c)]
+                add(block, block, first.at[0, 0, k, rows(c)], held.at[0, 0, k, rows(c)])
+                if k:
+                    z_copy(c, 1).start()
+            yx_copy(c).wait_recv()
+            for k in range(2):
+                block = second.at[1, k, rows(c)]
+                add(block, block, first.at[1, 0, k, rows(c)], held.at[0, 0, 2 + k, rows(c)])
+                z_copy(c, 2 + k).start()
+        elif s == 4:
+            for k in range(1, RING):
+                z_copy(c, k).wait_recv()
+            add(
+                total.at[rows(c)],
+                second.at[0, 0, rows(c)],
+                *(far.at[k, rows(c)] for k in range(3)),
+            )
+            out_own(c).start()
+            for q in (2, 4, 6, 1):
+                out_copy(c, q).start()
+        elif s == 5:
+            for q in (2, 4, 6):
+                out_copy_wait(c, q)
+                share_copy(c, q).start()
+
+    def out_copy_wait(c, q):
+        remote(
+            total.at[rows(c)], outs[c].at[turned(p, q)], send.at[c, 7 + q], recv.at[c, 7 + q], near(q)
+        ).wait_recv()
+
+    vec_in = pltpu.make_async_copy(vector_in, vec, local_sem.at[4, 0])
+    vec_out = pltpu.make_async_copy(vec.at[0], vector_out, local_sem.at[4, 1])
+
+    def vec_copy(i):
+        return remote(vec, vec_far.at[i], vec_send.at[i], vec_recv.at[i], near((1, 2, 4)[i]))
+
+    def vec_z(d):
+        return remote(
+            vec.at[shifts[d]], vec_far.at[3, d], vec_send.at[2 + d], vec_recv.at[2 + d], (p, shifts[d])
+        )
+
+    vec_in.start()
+    stage(0, 0)
+    stage(1, 0)
+    stage(2, 0)
+    stage(3, 0)
+    row_start(0, block_in, block_out)
+    row_start(1, grad_in, grad_out)
+    vec_in.wait()
+    vec_copy(0).start()
+    for t in range(1, 9):
+        for c in range(4):
+            if 1 <= t - c <= 5:
+                stage(c, t - c)
+        if 1 <= t <= 3:
+            vec_copy(t - 1).wait()
+            vec[...] = vec[...] + vec_far[t - 1]
+            if t < 3:
+                vec_copy(t).start()
+            else:
+                for d in range(1, RING):
+                    vec_z(d).start()
+        if t == 4:
+            for d in range(1, RING):
+                vec_z(d).wait()
+            vec[0] = vec[z] + (vec_far[3, 1] + (vec_far[3, 2] + vec_far[3, 3]))
+            vec_out.start()
+    for c in range(4):
+        out_copy_wait(c, 1)
+        for q in (2, 4, 6):
+            share_wait(c, q).wait_recv()
+        core_copy(c).wait_send()
+        x_copy(c).wait_send()
+        y_copy(c).wait_send()
+        xy_copy(c).wait_send()
+        yx_copy(c).wait_send()
+        for k in range(1, RING):
+            z_copy(c, k).wait_send()
+        for q in (2, 4, 6, 1):
+            out_copy(c, q).wait_send()
+        for q in (2, 4, 6):
+            share_copy(c, q).wait_send()
+        out_own(c).wait()
+    vec_out.wait()
+    row_wait(0, block_in, block_out)
+    row_wait(1, grad_in, grad_out)
+
+
+def reduce_all(images, block, grad, vectors, g2, g1, go, ga):
+    rows, full = block.shape
+    width = full // RING
+    sizes = tuple(g.shape[4] for g in (g2, g1, go, ga))
+    every = sum(sizes)
+    bf16 = jnp.bfloat16
+    f32 = jnp.float32
+    dma = pltpu.SemaphoreType.DMA
+    outs = [jax.ShapeDtypeStruct((images, rows, width), bf16)] * 2
+    outs.append(jax.ShapeDtypeStruct(vectors.shape[1:], f32))
+    outs += [jax.ShapeDtypeStruct((8, n, full), bf16) for n in sizes]
+    return pl.pallas_call(
+        functools.partial(reduce_kernel, images, sizes),
+        out_shape=outs,
+        in_specs=[pl.BlockSpec(memory_space=pl.ANY)] * 7,
+        out_specs=[pl.BlockSpec(memory_space=pl.ANY)] * 7,
+        scratch_shapes=[
+            pltpu.VMEM((2, 2, RING, every, full), bf16),
+            pltpu.VMEM((2, 2, RING, every, full), bf16),
+            pltpu.VMEM((2, 2, 2, every, full), bf16),
+            pltpu.VMEM((2, 2, every, full), bf16),
+            pltpu.VMEM((3, every, full), bf16),
+            pltpu.VMEM((every, full), bf16),
+            pltpu.VMEM(vectors.shape, f32),
+            pltpu.VMEM((4,) + vectors.shape, f32),
+            dma((4, 16)),
+            dma((4, 16)),
+            dma((2, RING)),
+            dma((2, RING)),
+            dma((6,)),
+            dma((6,)),
+            dma((5, 2)),
+        ],
+        compiler_params=pltpu.CompilerParams(
+            collective_id=1, has_side_effects=True, vmem_limit_bytes=56 * 2**20
+        ),
+    )(block, grad, vectors, g2, g1, go, ga)
+
+
+def low(value):
+    return value.astype(jnp.bfloat16)
+
+
+def wide(value):
+    return value.astype(jnp.float32)
+
+
+def pick(stack, index):
+    return lax.dynamic_index_in_dim(stack, index, 0, keepdims=False)
+
+
+def norm_full(value):
+    middle = jnp.mean(value, 1, keepdims=True)
+    spread = jnp.mean(value * value, 1, keepdims=True) - middle * middle
+    inverse = lax.rsqrt(spread + EPS)
+    return (value - middle) * inverse, inverse
+
+
+def norm_back(gradient, normalized, gain, inverse):
+    scaled = gradient * gain
+    first = jnp.mean(scaled, 1, keepdims=True)
+    second = jnp.mean(scaled * normalized, 1, keepdims=True)
+    return inverse * (scaled - first - normalized * second)
+
+
+def image_local(
+    tokens,
+    image_mask,
+    ln1_gain,
+    first_norm_bias,
+    w_attn,
+    qv_bias,
+    w_out,
+    b_out,
+    ln2_gain,
+    second_norm_bias,
+    w_fc1,
+    b_fc1,
+    w_fc2,
+    b_fc2,
+    cotangent,
+):
+    images, seq, width = tokens.shape
+    full = width * RING
+    heads = full // HD
+    p = lax.axis_index("dp")
+    z = lax.axis_index("tensor")
+    core = p % 2
+    slot = z - core
+    live = (slot >= 0) & (slot < images)
+    mask = jnp.where(
+        live, lax.dynamic_index_in_dim(image_mask, jnp.clip(slot, 0, images - 1), 0, False), 0
+    ).astype(jnp.float32)
+    rows = PAD
+
+    attn_pieces = (
+        jnp.transpose(w_attn, (1, 2, 0))
+        .reshape(3, 8, 32, full)
+        .transpose(1, 0, 2, 3)
+    )
+    out_pieces = w_out.reshape(8, 32, full)
+    fc1_pieces = jnp.transpose(w_fc1).reshape(8, -1, full)
+    fc2_pieces = w_fc2.reshape(8, -1, full)
+    hid = fc1_pieces.shape[1]
+    small = jnp.concatenate(
+        [
+            ln1_gain,
+            first_norm_bias,
+            b_out,
+            ln2_gain,
+            second_norm_bias,
+            b_fc2,
+            qv_bias.reshape(-1),
+            b_fc1,
+        ]
+    ).reshape(3, full)
+    small = jnp.pad(small, ((0, 13), (0, 0)))
+    tail = ((0, 0), (0, rows - seq), (0, 0))
+    x_rows, dy_rows, small_k, w_qkv, w_o, w_1, w_2 = gather_all(
+        jnp.pad(tokens, tail),
+        jnp.pad(cotangent, tail),
+        small,
+        attn_pieces,
+        out_pieces,
+        fc1_pieces,
+        fc2_pieces,
+    )
+    block_inputs = jnp.where(live, wide(x_rows), 0.0)
+    output_gradient = jnp.where(mask > 0, wide(dy_rows), 0.0)
+    w_qkv = w_qkv.reshape(3, full, full)
+    w_o = w_o.reshape(full, full)
+    w_1 = w_1.reshape(-1, full)
+    w_2 = w_2.reshape(-1, full)
+
+    small_k = small_k[:, :3].reshape(RING, -1)
+    small_j = jnp.stack([pick(small_k, (z - j) % RING) for j in range(RING)])
+
+    def feature_vector(i):
+        return wide(small_j[:, i * width : (i + 1) * width].reshape(full))
+
+    first_norm_gain, first_bias, out_bias, second_norm_gain, second_bias, fc2_bias = (
+        feature_vector(i) for i in range(6)
+    )
+
+    def relative(value):
+        value = jnp.swapaxes(value, 0, 1)
+        return jnp.stack([pick(value, p ^ q) for q in range(8)])
+
+    def natural(value):
+        value = jnp.stack([pick(value, r ^ p) for r in range(8)])
+        value = jnp.swapaxes(value, 0, 1)
+        return jnp.stack([pick(value, (z - j) % RING) for j in range(RING)])
+
+    def heads_of(value):
+        return value.reshape(4, 2, RING, 32).transpose(0, 2, 1, 3).reshape(-1)
+
+    def heads_back(value):
+        return value.reshape(4, RING, 2, 32).transpose(0, 2, 1, 3).reshape(8, RING, 32)
+
+    qv_k = small_k[:, 6 * width : 8 * width].reshape(RING, 2, 8, 32)
+    query_bias = wide(heads_of(relative(qv_k[:, 0])))
+    value_bias = wide(heads_of(relative(qv_k[:, 1])))
+    fc1_bias = wide(relative(small_k[:, 8 * width :].reshape(RING, 8, hid)).reshape(-1))
+
+    first_hat, first_inverse = norm_full(block_inputs)
+    h1 = low(first_hat * first_norm_gain + first_bias)
+    query = low(back_dot(h1, w_qkv[0]) + query_bias)[:seq].reshape(seq, heads, HD)
+    keys = low(back_dot(h1, w_qkv[1]))[:seq].reshape(seq, heads, HD)
+    values = low(back_dot(h1, w_qkv[2]) + value_bias)[:seq].reshape(seq, heads, HD)
+    context, log_total = attend_image((query, keys, values))
+    short = ((0, rows - seq), (0, 0))
+    context_flat = jnp.pad(context.reshape(seq, full), short)
+    attn = jnp.dot(context_flat, w_o, preferred_element_type=jnp.float32) + out_bias
+    residual = block_inputs + attn
+    second_hat, second_inverse = norm_full(residual)
+    h2 = low(second_hat * second_norm_gain + second_bias)
+    hidden = back_dot(h2, w_1) + fc1_bias
+    sigma = jax.nn.sigmoid(1.702 * hidden)
+    act = low(hidden * sigma)
+    slope = sigma + 1.702 * hidden * sigma * (1.0 - sigma)
+    mlp = jnp.dot(act, w_2, preferred_element_type=jnp.float32) + fc2_bias
+    block = low((residual + mlp) * mask)
+
+    dy = low(output_gradient)
+    grad_2 = low(pair_dot(act, dy)).reshape(2, 2, 2, RING, hid, full)
+    dhidden = low(back_dot(dy, w_2) * slope)
+    grad_1 = low(pair_dot(dhidden, h2)).reshape(2, 2, 2, RING, hid, full)
+    dh2 = jnp.dot(dhidden, w_1, preferred_element_type=jnp.float32)
+    second_gain_sum = jnp.sum(dh2 * second_hat, 0)
+    second_bias_sum = jnp.sum(dh2, 0)
+    residual_gradient = output_gradient + norm_back(
+        dh2, second_hat, second_norm_gain, second_inverse
+    )
+    dattn = low(residual_gradient)
+    dcontext = low(back_dot(dattn, w_o))
+
+    def head_pieces(grad, count):
+        grad = grad.reshape(count, 4, RING, 2, 32, full).transpose(1, 3, 2, 0, 4, 5)
+        return grad.reshape(2, 2, 2, RING, count * 32, full)
+
+    grad_o = head_pieces(low(pair_dot(context_flat, dattn)), 1)
+    dqkv = attend_back((query, keys, values, log_total, dcontext[:seq].reshape(seq, heads, HD)))
+    dqkv = jnp.pad(dqkv.reshape(seq, 3 * full), short)
+    grad_a = head_pieces(low(pair_dot(dqkv, h1)), 3)
+    dh1 = jnp.dot(dqkv, w_qkv.reshape(3 * full, full), preferred_element_type=jnp.float32)
+    first_gain_sum = jnp.sum(dh1 * first_hat, 0)
+    first_bias_sum = jnp.sum(dh1, 0)
+    grad = low(residual_gradient + norm_back(dh1, first_hat, first_norm_gain, first_inverse))
+
+    qkv_sums = jnp.sum(dqkv, 0, dtype=jnp.float32).reshape(3, full)
+    vectors = jnp.concatenate(
+        [
+            v.reshape(RING, -1)
+            for v in (
+                first_gain_sum,
+                first_bias_sum,
+                jnp.sum(dattn, 0, dtype=jnp.float32),
+                second_gain_sum,
+                second_bias_sum,
+                jnp.sum(output_gradient, 0),
+                natural(heads_back(qkv_sums[0])),
+                natural(heads_back(qkv_sums[2])),
+                natural(jnp.sum(dhidden, 0, dtype=jnp.float32).reshape(8, RING, hid)),
+            )
+        ],
+        1,
+    ).reshape(RING, 24, 128)
+    block_out, input_grad, vectors, s2, s1, so, sa = reduce_all(
+        images, block, grad, vectors, grad_2, grad_1, grad_o, grad_a
+    )
+    vectors = vectors.reshape(-1)
+    sums = [vectors[i * width : (i + 1) * width] for i in range(6)]
+    return (
+        block_out[:, :seq],
+        input_grad[:, :seq],
+        sums[0],
+        sums[1],
+        jnp.transpose(wide(sa).reshape(8, 3, 32, full), (3, 1, 0, 2)).reshape(full, 3, width),
+        vectors[6 * width : 8 * width].reshape(2, width),
+        wide(so).reshape(width, full),
+        sums[2],
+        sums[3],
+        sums[4],
+        jnp.transpose(wide(s1).reshape(8 * hid, full)),
+        vectors[8 * width :],
+        wide(s2).reshape(8 * hid, full),
+        sums[5],
+    )
+
+
 def solution(mesh):
     in_specs = (
         P("dp", None, "tensor"),
@@ -269,4 +1051,13 @@
         P("tensor", None),
         P("tensor"),
     )
-    return jax.shard_map(local, mesh=mesh, in_specs=in_specs, out_specs=out_specs, check_vma=False)
+    owners = mesh.shape["dp"] == 8 and mesh.shape["tensor"] == RING
+
+    def block(*arrays):
+        images = arrays[0].shape[0] // mesh.shape["dp"]
+        body = image_local if owners and images < RING else local
+        return jax.shard_map(
+            body, mesh=mesh, in_specs=in_specs, out_specs=out_specs, check_vma=False
+        )(*arrays)
+
+    return block

time: 1180 us -> 680 us (0.58)
  waiting for transfers between devices: 825 us -> 0 us
  Pallas kernels: 0 us -> 391 us
  blocking collectives: 98.8 us -> 0 us
  matrix products: 114 us -> 165 us
  local copies, waits for them, and re-layouts: 75.8 us -> 60 us
  between operations: 14.4 us -> 2.5 us
    reduce_scatter x4 -> x0, waiting for transfers between devices: 432 us -> none  [settle_sums(): return lax.psum_scatter(value, 'tensor', scatter_dimension=1, tiled=True)]
    pallas_call x0 -> x2, Pallas kernels: none -> 391 us  [the longest x1 219 us: gather_all(): pl.pallas_call(functools.partial(gather_kernel, images), out_shape=[jax.S...]
    all_gather x4 -> x0, waiting for transfers between devices: 262 us -> none  [spread_features(): return lax.all_gather(value, 'tensor', axis=1, tiled=True)]
    psum x1 -> x0, waiting for transfers between devices: 131 us -> none  [local(): lax.psum((first_norm_gain_gradient, grad_ln1_bias, grad_w_attn, grad_qv_b...]
    psum x5 -> x0, blocking collectives: 98.8 us -> none  [the longest x2 38.6 us: norm_stats(): lax.psum((jnp.sum(value, 1), jnp.sum(value * value, 1)), 'tensor')]
    while x12 -> x0, local copies, waits for them, and re-layouts: 23.4 us -> none  [the longest x4 13.2 us: local(): context, log_total = lax.map(attend_image, (query, keys, values))]
    slice x5 -> x15, local copies, waits for them, and re-layouts: 1.55 us -> 22.6 us  [the longest x3 9.07 us: image_local(): keys = low(back_dot(h1, w_qkv[1]))[:seq].reshape(seq, heads, HD)]
    dot_general x3 -> x4, matrix products: 17.2 us -> 37.6 us  [pair_dot(): lax.dot_general(left, right, (((0,), (0,)), ((), ())), preferred_element_...]
  transfers between devices with their start and end apart: 9 -> 0, of which waited for: 9 -> 0; matrix products, arithmetic and copies ran while one was open for 5% -> 0% of each run, Pallas kernels for 0% -> 0%
where the time goes in v1:
time: 680 us; the launch traced here: 671 us
  Pallas kernels  391 us (58%)
  matrix products  165 us (24%)
  local copies, waits for them, and re-layouts  60 us (9%)
  other arithmetic  53.3 us (8%)
    pallas_call x1, Pallas kernels, gather_all(): pl.pallas_call(functools.partial(gather_kernel, images), out_shape=[jax.S...  219 us
    pallas_call x1, Pallas kernels, reduce_all(): pl.pallas_call(functools.partial(reduce_kernel, images, sizes), out_shape...  172 us
    dot_general x4, matrix products, pair_dot(): lax.dot_general(left, right, (((0,), (0,)), ((), ())), preferred_element_...  37.6 us
    dot_general x6, matrix products, back_dot(): lax.dot_general(left, right, (((1,), (1,)), ((), ())), preferred_element_...  33.6 us
    convert_element_type x1, other arithmetic, attend_back(): dscores = (probs * (dprobs - delta)).astype(jnp.bfloat16)  20.2 us
    dot_general x1, matrix products, attend_back(): jnp.einsum('qhd,khd->hqk', dcontext, values, preferred_element_type=jnp.f...  15.1 us

profile of v1, /device:TPU:0, one launch (start us, length us, event | category | flops | bytes accessed | tf_op | source)
XLA Modules:
  0.0 671.1 jit_solution(15972702344043610039)
XLA Ops:
  0.8 1.4 dynamic_slice.207
  10.1 2.2 pad.19.tokens
  14.1 1.3 copy.149
  15.4 3.9 copy.74
  19.3 219.0 %shard_map.254 = (bf16[592,1024]{1,0:T(8,128)(2,1)}, bf16[592,1024]{1,0:T(8,128)(2,1)}, bf16[4,16,1024]{2,1,0:T(8,128)(2,1)}, bf16[3,4,4,2,32,1024]{5,4,3,2,1,0:...) custom-call(bf16[3,592,256]{2,1,0:T(8,128)(2,1)} %pad.19.tokens, ...), custom_call_target="tpu_custom_call" | custom-call | tf_op jit(solution)/shard_map/pallas_call | solution.py:449
  239.3 1.8 fusion.12
  241.9 6.3 fusion.56
  248.2 1.5 fusion.52
  250.8 1.7 copy.79
  252.5 3.5 fusion.53
  256.1 1.3 fusion.13
  257.4 1.7 copy.78
  259.1 3.9 fusion.54
  263.0 1.3 fusion.14
  264.3 2.4 copy.76
  266.7 10.3 %multiply_reduce_fusion.1 = (f32[16,577]{1,0:T(8,128)S(1)}, f32[16,577,577]{1,2,0:T(8,128)}) fusion(bf16[577,16,64]{0,2,1:T(8,128)(2,1)S(1)} %bitcast.249, bf16[577,16,64]{0,2,1:T(8,128)(2,1)S(1)} %bitcast.244), kind=kOutput, calls=%fused_computation.6 | convolution fusion | flops 692483072 | bytes 23707776 | tf_op jit(solution)/shard_map/qhd,khd->hqk/dot_general | solution.py:60
  277.0 11.0 %fusion = f32[16,577]{1,0:T(8,128)S(1)} fusion(f32[16,577,577]{1,2,0:T(8,128)} %get-tuple-element.157, f32[16,577]{1,0:T(8,128)S(1)} %get-tuple-element.156), kind=kLoop, calls=%fused_computation.5 | loop fusion | flops 15971360 | bytes 21381312 | tf_op jit(solution)/shard_map/reduce_sum | solution.py:63
  288.7 11.5 %fusion.18 = bf16[16,64,577]{2,1,0:T(8,128)(2,1)} fusion(bf16[577,16,64]{0,2,1:T(8,128)(2,1)S(1)} %bitcast.261, f32[16,577,577]{1,2,0:T(8,128)} %get-tuple-element.157, f32[16,577]{1,0:T(8,128)S(1)} %fusion, f32[16,577]{1,0:T(8,128)S(1)} %get-tuple-element.156), kind=kOutput, calls=%fused_computation.58 | convolution fusion | flops 703736896 | bytes 23744704 | tf_op jit(solution)/shard_map/hqk,khd->qhd/dot_general | solution.py:66
  300.2 3.9 fusion.55
  304.2 8.0 %fusion.51 = f32[592,4096]{1,0:T(8,128)} fusion(bf16[4096,1024]{1,0:T(8,128)(2,1)S(1)} %bitcast.316, f32[592,1024]{1,0:T(8,128)S(1)} %get-tuple-element.158, f32[1024]{0:T(1024)S(1)} %bitcast.308, f32[1024]{0:T(1024)S(1)} %bitcast.289, f32[592]{0:T(1024)S(1)} %get-tuple-element.153, f32[592]{0:T(1024)S(1)} %get-tuple-element.152), kind=kOutput, calls=%fused_computation.225 | convolution fusion | flops 4969086976 | bytes 20525696 | tf_op jit(solution)/shard_map/dot_general | solution.py:52
  312.1 11.6 %multiply_convert_fusion.5.refs_0_ = bf16[592,1024]{1,0:T(8,128)(2,1)} fusion(f32[592,1024]{1,0:T(8,128)S(1)} %get-tuple-element.158, bf16[4096,1024]{1,0:T(8,128)(2,1)} %bitcast.320, f32[]{:T(128)S(6)} %convert_element_type.233, f32[1024]{0:T(1024)S(1)} %bitcast.310, f32[592,4096]{1,0:T(8,128)} %fusion.51, f32[4096]{0:T(1024)S(1)} %convert.40), kind=kOutput, calls=%fused_computation.36 | convolution fusion | flops 4985454592 | bytes 21745668 | tf_op jit(solution)/shard_map/dot_general | solution.py:950
  323.7 15.3 %convert_reduce_fusion = (f32[4096]{0:T(1024)S(1)}, bf16[592,4096]{1,0:T(8,128)(2,1)}) fusion(f32[592,4096]{1,0:T(8,128)} %fusion.51, f32[4096]{0:T(1024)S(1)} %convert.40, bf16[4096,1024]{1,0:T(8,128)(2,1)} %bitcast.321, bf16[592,1024]{1,0:T(8,128)(2,1)S(1)} %copy-done.18, pred[]{:T(512)S(6)} %gt.3), kind=kOutput, calls=%fused_computation.12 | convolution fusion | flops 4999393280 | bytes 24182784 | tf_op jit(solution)/shard_map/dot_general | solution.py:52
  339.0 14.1 %convolution_convert_fusion.1 = bf16[4096,1024]{1,0:T(8,128)(2,1)} fusion(bf16[592,1024]{1,0:T(8,128)(2,1)S(1)} %copy-done.18, pred[]{:T(512)S(6)} %gt.3, f32[592,4096]{1,0:T(8,128)} %fusion.51, f32[4096]{0:T(1024)S(1)} %convert.40), kind=kOutput, calls=%fused_computation.18 | convolution fusion | flops 4989042688 | bytes 19316736 | tf_op jit(solution)/shard_map/dot_general | solution.py:46
  353.1 7.1 %multiply_reduce_fusion.2 = (f32[1024]{0:T(1024)S(1)}, f32[592]{0:T(1024)S(1)}, f32[592]{0:T(1024)S(1)}, f32[1024]{0:T(1024)S(1)}, f32[592,1024]{1,0:T(8,128)}) fusion(f32[592,1024]{1,0:T(8,128)S(1)} %get-tuple-element.158, f32[592]{0:T(1024)S(1)} %get-tuple-element.153, f32[592]{0:T(1024)S(1)} %get-tuple-element.152, f32[1024]{0:T(1024)S(1)} %bitcast.290, ...), kind=kOutput, calls=%fused_computation.26 | convolution fusion | flops 4971508736 | bytes 18109696 | tf_op jit(solution)/shard_map/dot_general | solution.py:957
  360.2 3.1 convert_reduce_fusion.2
  363.4 1.5 fusion.41
  366.2 1.7 copy.89
  367.9 3.9 convolution_convert_fusion.3
  371.8 1.5 copy.95
  374.2 12.0 %convolution_convert_fusion = bf16[4096,1024]{1,0:T(8,128)(2,1)} fusion(bf16[592,4096]{1,0:T(8,128)(2,1)} %get-tuple-element.164, f32[592,1024]{1,0:T(8,128)S(1)} %copy-done.15, f32[1024]{0:T(1024)S(1)} %bitcast.309, f32[1024]{0:T(1024)S(1)} %bitcast.292, f32[592]{0:T(1024)S(1)} %get-tuple-element.153, f32[592]{0:T(1024)S(1)} %get-tuple-element.152), kind=kOutput, calls=%fused_computation.17 | convolution fusion | flops 4973281280 | bytes 15676032 | tf_op jit(solution)/shard_map/dot_general | solution.py:46
  386.2 13.0 %fusion.21 = bf16[577,1,16,64]{0,3,2,1:T(8,128)(2,1)} fusion(bf16[577,16,64]{0,2,1:T(8,128)(2,1)S(1)} %bitcast.247, f32[16,577,577]{1,2,0:T(8,128)} %get-tuple-element.157, f32[16,577]{1,0:T(8,128)S(1)} %copy-done.21), kind=kOutput, calls=%fused_computation.62 | convolution fusion | flops 698410048 | bytes 23707776 | tf_op jit(solution)/shard_map/hqk,qhd->khd/dot_general | solution.py:77
  399.2 15.1 %multiply_reduce_fusion = (f32[16,577]{1,0:T(8,128)S(1)}, f32[16,577,577]{1,2,0:T(8,128)}) fusion(f32[16,577,577]{1,2,0:T(8,128)} %get-tuple-element.157, f32[16,577]{1,0:T(8,128)S(1)} %copy-done.21, bf16[577,16,64]{0,2,1:T(8,128)(2,1)S(1)} %bitcast.248, bf16[577,16,64]{0,2,1:T(8,128)(2,1)S(1)} %bitcast.262), kind=kOutput, calls=%fused_computation.1 | convolution fusion | flops 703136768 | bytes 45052160 | tf_op jit(solution)/shard_map/qhd,khd->hqk/dot_general | solution.py:80
  414.2 20.2 %multiply_convert_fusion = bf16[16,577,577]{1,2,0:T(8,128)(2,1)} fusion(f32[16,577,577]{1,2,0:T(8,128)} %get-tuple-element.161, f32[16,577,577]{1,2,0:T(8,128)} %get-tuple-element.157, f32[16,577]{1,0:T(8,128)S(1)} %get-tuple-element.160, f32[16,577]{1,0:T(8,128)S(1)} %copy-done.21), kind=kLoop, calls=%fused_computation | loop fusion | flops 26634320 | bytes 53342496 | tf_op jit(solution)/shard_map/convert_element_type | solution.py:82
  434.4 8.2 %fusion.20 = bf16[577,1,16,64]{0,3,2,1:T(8,128)(2,1)S(1)} fusion(bf16[577,16,64]{0,2,1:T(8,128)(2,1)S(1)} %bitcast.250, bf16[16,577,577]{1,2,0:T(8,128)(2,1)} %multiply_convert_fusion), kind=kOutput, calls=%fused_computation.61 | convolution fusion | flops 683020288 | bytes 13017120 | tf_op jit(solution)/shard_map/hqk,qhd->khd/dot_general | solution.py:84
  442.6 6.8 %fusion.19 = bf16[577,1,16,64]{0,3,2,1:T(8,128)(2,1)S(1)} fusion(bf16[577,16,64]{0,2,1:T(8,128)(2,1)S(1)} %bitcast.245, bf16[16,577,577]{1,2,0:T(8,128)(2,1)} %multiply_convert_fusion), kind=kOutput, calls=%fused_computation.60 | convolution fusion | flops 683020288 | bytes 13017120 | tf_op jit(solution)/shard_map/hqk,khd->qhd/dot_general | solution.py:83
  450.8 6.2 multiply_reduce_fusion.3
  457.0 4.1 add_convert_fusion.refs_1_
  463.6 7.7 %convolution_convert_fusion.2 = bf16[3072,1024]{1,0:T(8,128)(2,1)S(1)} fusion(bf16[577,3072]{0,1:T(8,128)(2,1)} %bitcast.242, bf16[592,1024]{1,0:T(8,128)(2,1)S(1)} %copy-done.13, f32[1024]{0:T(1024)S(1)} %bitcast.307, f32[1024]{0:T(1024)S(1)} %bitcast.288, f32[592]{0:T(1024)S(1)} %copy-done.28, f32[592]{0:T(1024)S(1)} %copy-done.26, pred[]{:T(512)S(6)} %and.39), kind=kOutput, calls=%fused_computation.19 | convolution fusion | flops 3731931136 | bytes 11061889 | tf_op jit(solution)/shard_map/dot_general | solution.py:46
  471.3 3.4 copy.96
  474.6 171.6 %shard_map.255 = (bf16[3,592,256]{2,1,0:T(8,128)(2,1)}, bf16[3,592,256]{2,1,0:T(8,128)(2,1)}, f32[24,128]{1,0:T(8,128)}, bf16[8,128,1024]{2,1,0:T(8,128)(2,1)}, ...) custom-call(bf16[592,1024]{1,0:T(8,128)(2,1)} %multiply_convert_fusion.5.refs_0_, ...), custom_call_target="tpu_custom_call" | custom-call | tf_op jit(solution)/shard_map/pallas_call | solution.py:781
  646.2 2.3 slice.153
  649.8 1.3 slice_bitcast_fusion.2
  651.0 1.4 slice_bitcast_fusion.3
  654.5 1.8 copy.97
  656.3 2.4 copy.99
  658.7 4.1 bitcast_convert_fusion.1
  662.8 5.5 copy.98
  668.3 2.6 bitcast_convert_fusion
  (198 shorter events, 21.8 us)
Async XLA Ops:
  0.6 11.6 %copy-start.19 = (bf16[3,577,256]{2,1,0:T(8,128)(2,1)S(1)}, bf16[3,577,256]{2,1,0:T(8,128)(2,1)}, u32[]{:S(2)}) copy-start(bf16[3,577,256]{2,1,0:T(8,128)(2,1)} %param.29) | copy-start | bytes 2658820
  0.7 12.5 %copy-start.17 = (bf16[1024,3,256]{2,0,1:T(8,128)(2,1)S(1)}, bf16[1024,3,256]{2,0,1:T(8,128)(2,1)}, u32[]{:S(2)}) copy-start(bf16[1024,3,256]{2,0,1:T(8,128)(2,1)} %param.19) | copy-start | bytes 4718596
  241.1 17.9 %copy-start.25 = (f32[592]{0:T(1024)}, f32[592]{0:T(1024)S(1)}, u32[]{:S(2)}) copy-start(f32[592]{0:T(1024)S(1)} %get-tuple-element.154) | copy-start | bytes 7108
  241.2 17.9 %copy-start.27 = (f32[592]{0:T(1024)}, f32[592]{0:T(1024)S(1)}, u32[]{:S(2)}) copy-start(f32[592]{0:T(1024)S(1)} %get-tuple-element.155) | copy-start | bytes 7108
  241.9 17.2 %copy-start.23 = (f32[1,2,4,128]{3,1,2,0:T(2,128)}, f32[1,2,4,128]{3,1,2,0:T(2,128)S(1)}, u32[]{:S(2)}) copy-start(f32[1,2,4,128]{3,1,2,0:T(2,128)S(1)} %copy.122) | copy-start | bytes 12292
  241.9 17.2 %copy-start.29 = (f32[1,2,4,128]{3,1,2,0:T(2,128)}, f32[1,2,4,128]{3,1,2,0:T(2,128)S(1)}, u32[]{:S(2)}) copy-start(f32[1,2,4,128]{3,1,2,0:T(2,128)S(1)} %copy.123) | copy-start | bytes 12292
  241.9 6.3 copy-start.10
  252.5 14.2 %copy-start.2 = (bf16[577,1024]{0,1:T(8,128)(2,1)}, bf16[577,1024]{0,1:T(8,128)(2,1)S(1)}, u32[]{:S(2)}) copy-start(bf16[577,1024]{0,1:T(8,128)(2,1)S(1)} %copy.79) | copy-start | bytes 3545092
  259.1 7.7 %copy-start.4 = (bf16[577,1024]{0,1:T(8,128)(2,1)}, bf16[577,1024]{0,1:T(8,128)(2,1)S(1)}, u32[]{:S(2)}) copy-start(bf16[577,1024]{0,1:T(8,128)(2,1)S(1)} %copy.78) | copy-start | bytes 3545092
  277.0 11.7 %copy-start.8 = (bf16[577,1024]{0,1:T(8,128)(2,1)S(1)}, bf16[577,1024]{0,1:T(8,128)(2,1)}, u32[]{:S(2)}) copy-start(bf16[577,1024]{0,1:T(8,128)(2,1)} %copy.76) | copy-start | bytes 3545092
  277.0 27.1 %slice-start.2 = ((s8[8388608]{0:T(1024)(128)(4,1)}), s8[4194304]{0:T(1024)(128)(4,1)S(1)}, s32[]{:S(2)}) async-start(s8[8388608]{0:T(1024)(128)(4,1)} %bitcast.314), calls=%async_computation.2 | async-start | bytes 8388608
  288.7 11.5 %copy-start.11 = (bf16[592,1024]{1,0:T(8,128)(2,1)S(1)}, bf16[592,1024]{1,0:T(8,128)(2,1)}, u32[]{:S(2)}) copy-start(bf16[592,1024]{1,0:T(8,128)(2,1)} %get-tuple-element.28) | copy-start | bytes 3637252
  288.7 15.4 %slice-start.3 = ((s8[8388608]{0:T(1024)(128)(4,1)}), s8[4194304]{0:T(1024)(128)(4,1)S(1)}, s32[]{:S(2)}) async-start(s8[8388608]{0:T(1024)(128)(4,1)} %bitcast.314), calls=%async_computation.3 | async-start | bytes 8388608
  304.1 49.0 %copy-start.14 = (f32[592,1024]{1,0:T(8,128)}, f32[592,1024]{1,0:T(8,128)S(1)}, u32[]{:S(2)}) copy-start(f32[592,1024]{1,0:T(8,128)S(1)} %get-tuple-element.158) | copy-start | bytes 7274500
  312.1 11.6 %copy-start.18 = (bf16[592,1024]{1,0:T(8,128)(2,1)S(1)}, bf16[592,1024]{1,0:T(8,128)(2,1)}, u32[]{:S(2)}) copy-start(bf16[592,1024]{1,0:T(8,128)(2,1)} %get-tuple-element.34) | copy-start | bytes 3637252
  312.1 41.0 %slice-start.4 = ((s8[8388608]{0:T(1024)(128)(4,1)}), s8[4194304]{0:T(1024)(128)(4,1)S(1)}, s32[]{:S(2)}) async-start(s8[8388608]{0:T(1024)(128)(4,1)} %bitcast.317), calls=%async_computation.4 | async-start | bytes 8388608
  323.7 29.4 %slice-start.5 = ((s8[8388608]{0:T(1024)(128)(4,1)}), s8[4194304]{0:T(1024)(128)(4,1)S(1)}, s32[]{:S(2)}) async-start(s8[8388608]{0:T(1024)(128)(4,1)} %bitcast.317), calls=%async_computation.5 | async-start | bytes 8388608
  339.0 14.1 %copy-start.32 = (bf16[592,4096]{1,0:T(8,128)(2,1)S(1)}, bf16[592,4096]{1,0:T(8,128)(2,1)}, u32[]{:S(2)}) copy-start(bf16[592,4096]{1,0:T(8,128)(2,1)} %get-tuple-element.164) | copy-start | bytes 14548996
  360.2 3.2 copy-start.31
  363.3 1.5 copy-start.6
  371.7 2.4 copy-start.15
  374.2 12.0 %copy-start.21 = (f32[16,577]{1,0:T(8,128)S(1)}, f32[16,577]{1,0:T(8,128)}, u32[]{:S(2)}) copy-start(f32[16,577]{1,0:T(8,128)} %log_add_fusion) | copy-start | bytes 110788
  414.2 20.2 %copy-start.5 = (bf16[577,1024]{0,1:T(8,128)(2,1)S(1)}, bf16[577,1024]{0,1:T(8,128)(2,1)}, u32[]{:S(2)}) copy-start(bf16[577,1024]{0,1:T(8,128)(2,1)} %copy-done.4) | copy-start | bytes 3545092
  434.4 8.2 %copy-start.3 = (bf16[577,1024]{0,1:T(8,128)(2,1)S(1)}, bf16[577,1024]{0,1:T(8,128)(2,1)}, u32[]{:S(2)}) copy-start(bf16[577,1024]{0,1:T(8,128)(2,1)} %copy-done.2) | copy-start | bytes 3545092
  434.4 16.2 %slice-start = ((s8[6291456]{0:T(1024)(128)(4,1)}), s8[2097152]{0:T(1024)(128)(4,1)S(1)}, s32[]{:S(2)}) async-start(s8[6291456]{0:T(1024)(128)(4,1)} %bitcast.255), calls=%async_computation | async-start | bytes 4194304
  442.6 6.8 %copy-start.9 = (bf16[577,1,16,64]{0,3,2,1:T(8,128)(2,1)S(1)}, bf16[577,1,16,64]{0,3,2,1:T(8,128)(2,1)}, u32[]{:S(2)}) copy-start(bf16[577,1,16,64]{0,3,2,1:T(8,128)(2,1)} %fusion.21) | copy-start | bytes 3545092
  442.6 8.0 %slice-start.1 = ((s8[6291456]{0:T(1024)(128)(4,1)}), s8[4194304]{0:T(1024)(128)(4,1)S(1)}, s32[]{:S(2)}) async-start(s8[6291456]{0:T(1024)(128)(4,1)} %bitcast.255), calls=%async_computation.1 | async-start | bytes 8388608
  449.5 1.3 copy-start.12
  449.5 1.3 copy-start.24
  449.5 1.3 copy-start.26
  449.5 1.3 copy-start.28
  450.6 6.3 copy-start
  450.8 6.2 copy-start.7
  457.0 4.1 copy-start.1
  461.1 2.5 copy-start.13
  461.1 2.5 copy-start.30
  646.2 6.2 copy-start.20
  646.2 7.2 %copy-start.22 = (bf16[8,32,1024]{2,1,0:T(8,128)(2,1)S(1)}, bf16[8,32,1024]{2,1,0:T(8,128)(2,1)}, u32[]{:S(2)}) copy-start(bf16[8,32,1024]{2,1,0:T(8,128)(2,1)} %get-tuple-element.39) | copy-start | bytes 1572868
  662.8 5.5 copy-start.16

commit v2 on v0

--- a/solution.py
+++ b/solution.py
@@ -1,6 +1,10 @@
+import functools
+
 import jax
 import jax.numpy as jnp
 from jax import lax
+from jax.experimental import pallas as pl
+from jax.experimental.pallas import tpu as pltpu
 from jax.sharding import PartitionSpec as P
 
 MODEL_WIDTH = 1024
@@ -235,6 +239,1455 @@
     )
 
 
+RING = 4
+
+
+MESH_ID = pl.DeviceIdType.MESH
+ROWS = 640
+TILE = 512
+
+
+def low(value):
+    return value.astype(jnp.bfloat16)
+
+
+def wide(value):
+    return value.astype(jnp.float32)
+
+
+def dot_on(left, right, a, b):
+    return lax.dot_general(
+        left, right, (((a,), (b,)), ((), ())), preferred_element_type=jnp.float32
+    )
+
+
+def turned(p, q):
+    return sum(lax.rem(p // bit + q // bit, 2) * bit for bit in (1, 2, 4))
+
+
+def remote(src, dst, send, recv, target):
+    return pltpu.make_async_remote_copy(
+        src_ref=src,
+        dst_ref=dst,
+        send_sem=send,
+        recv_sem=recv,
+        device_id=target,
+        device_id_type=MESH_ID,
+    )
+
+
+def rows_at(start, size):
+    return pl.ds(pl.multiple_of(start, 16), size)
+
+
+class Place:
+    def __init__(self, images):
+        self.p = lax.axis_index("dp")
+        self.z = lax.axis_index("tensor")
+        self.core = lax.rem(self.p, 2)
+        self.images = images
+        self.shifts = [lax.rem(self.z + d, RING) for d in range(RING)]
+        self.slot = self.z - self.core
+        self.live = self.holds(self.z)
+
+    def holds(self, plane):
+        return (plane - self.core >= 0) & (plane - self.core < self.images)
+
+    def near(self, q):
+        return (turned(self.p, q), self.z)
+
+    def greet(self):
+        barrier = pltpu.get_barrier_semaphore()
+        for d in range(1, RING):
+            pl.semaphore_signal(
+                barrier, inc=1, device_id=(self.p, self.shifts[d]), device_id_type=MESH_ID
+            )
+        for q in (1, 2, 4, 6):
+            pl.semaphore_signal(barrier, inc=1, device_id=self.near(q), device_id_type=MESH_ID)
+        pl.semaphore_wait(barrier, 7)
+
+
+def weight_copies(place, pieces, full, chunk, target, sem, c=0, q=0):
+    if chunk >= 2:
+        yield pltpu.make_async_copy(
+            pieces.at[turned(place.p, q)], target.at[pl.ds(0, 128)], sem
+        )
+        yield pltpu.make_async_copy(full.at[q], target.at[pl.ds(128, 384)], sem)
+        return
+    for half in range(2):
+        source = full.at[c, half] if chunk == 0 else full.at[half]
+        yield pltpu.make_async_copy(source, target.at[pl.ds(half * TILE + 128, 384)], sem)
+        for head in range(4):
+            own = pieces.at[turned(place.p, 2 * head + half)]
+            if chunk == 0:
+                own = own.at[c]
+            yield pltpu.make_async_copy(own, target.at[pl.ds(half * TILE + head * 32, 32)], sem)
+
+
+class Gather:
+    def __init__(self, place, pieces, fulls, sems):
+        self.at = place
+        self.p, self.z = place.p, place.z
+        self.pieces = pieces
+        self.fulls = fulls
+        self.z_send, self.send, self.recv = sems
+        z = self.z
+        self.order = (
+            jnp.where(z == 0, 3, 1),
+            jnp.where((z == 0) | (z == 3), 2, 3),
+            jnp.where(z == 0, 1, jnp.where(z == 3, 3, 2)),
+        )
+
+    def place(self, chunk, q, k, start=0, size=None):
+        full = self.fulls[chunk]
+        size = self.pieces[chunk].shape[-2] if size is None else size
+        start = (k - 1) * 128 + start
+        if chunk >= 2:
+            return full.at[q, rows_at(start, size)]
+        at = rows_at(start + (q // 2) * 32, size)
+        return full.at[:, q % 2, at] if chunk == 0 else full.at[q % 2, at]
+
+    def part(self, chunk, q, k, side):
+        half = self.pieces[chunk].shape[-2] // 2
+        return self.place(chunk, q, k, side * half, half)
+
+    def up(self, chunk, k, source):
+        return remote(
+            source,
+            self.place(chunk, 0, k + 1),
+            self.z_send.at[chunk, k, 0],
+            self.recv.at[chunk, k + 1, 0],
+            (self.p, jnp.minimum(self.z + 1, RING - 1)),
+        )
+
+    def down(self, chunk, k, source):
+        return remote(
+            source,
+            self.place(chunk, 0, k - 1),
+            self.z_send.at[chunk, lax.rem(k, RING), 1],
+            self.recv.at[chunk, k - 1, 0],
+            (self.p, jnp.maximum(self.z - 1, 0)),
+        )
+
+    def z_start(self, chunk):
+        piece = self.pieces[chunk].at[self.p]
+        pl.when(self.z < RING - 1)(self.up(chunk, 0, piece).start)
+        pl.when(self.z > 0)(self.down(chunk, RING, piece).start)
+
+    def z_sent(self, chunk):
+        piece = self.pieces[chunk].at[self.p]
+        pl.when(self.z < RING - 1)(self.up(chunk, 0, piece).wait_send)
+        pl.when(self.z > 0)(self.down(chunk, RING, piece).wait_send)
+        for k in (1, 2, 3):
+            here = self.place(chunk, 0, k)
+            if k < 3:
+                pl.when((self.z >= k) & (self.z < RING - 1))(self.up(chunk, k, here).wait_send)
+            if k > 1:
+                pl.when((self.z < k) & (self.z > 0))(self.down(chunk, k, here).wait_send)
+
+    def plane(self, chunk, k, source, target):
+        return remote(
+            self.place(chunk, source, k),
+            self.place(chunk, target, k),
+            self.send.at[chunk, k, target],
+            self.recv.at[chunk, k, target],
+            self.at.near(source ^ target),
+        )
+
+    def corner(self, chunk, k, side):
+        source, flip = ((4, 2), (2, 4))[side]
+        return remote(
+            self.part(chunk, source, k, side),
+            self.part(chunk, 6, k, side),
+            self.send.at[chunk, k, (6, 8)[side]],
+            self.recv.at[chunk, k, (6, 8)[side]],
+            self.at.near(flip),
+        )
+
+    def spread(self, chunk, i):
+        k = self.order[i]
+        here = self.place(chunk, 0, k)
+        remote(
+            here, here, self.send.at[chunk, k, 0], self.recv.at[chunk, k, 0], self.at.near(1)
+        ).wait_recv()
+        pl.when((self.z >= k) & (self.z < RING - 1))(self.up(chunk, k, here).start)
+        pl.when((self.z < k) & (self.z > 0))(self.down(chunk, k, here).start)
+        for target in (2, 4, 1):
+            self.plane(chunk, k, 0, target).start()
+
+    def relay(self, chunk, i):
+        k = self.order[i]
+        self.plane(chunk, k, 0, 4).wait_recv()
+        self.corner(chunk, k, 0).start()
+        self.plane(chunk, k, 0, 2).wait_recv()
+        self.corner(chunk, k, 1).start()
+        self.plane(chunk, k, 4, 5).start()
+        self.plane(chunk, k, 2, 3).start()
+
+    def share(self, chunk, i):
+        k = self.order[i]
+        self.corner(chunk, k, 0).wait_recv()
+        self.corner(chunk, k, 1).wait_recv()
+        self.plane(chunk, k, 6, 7).start()
+
+    def whole(self, chunk):
+        for k in range(1, RING):
+            for target in (1, 3, 5, 7):
+                self.plane(chunk, k, target - 1, target).wait_recv()
+
+    def sent(self, chunk):
+        self.z_sent(chunk)
+        for k in range(1, RING):
+            for source, target in ((0, 2), (0, 4), (0, 1), (4, 5), (2, 3), (6, 7)):
+                self.plane(chunk, k, source, target).wait_send()
+            self.corner(chunk, k, 0).wait_send()
+            self.corner(chunk, k, 1).wait_send()
+
+
+class Rows:
+    def __init__(self, place, source, target, send, recv, local):
+        self.at = place
+        self.source, self.target = source, target
+        self.send, self.recv, self.local = send, recv, local
+        self.width = source.shape[2]
+
+    def columns(self):
+        return pl.ds(pl.multiple_of(self.at.z * self.width, self.width), self.width)
+
+    def copy(self, d):
+        dest = self.at.shifts[d]
+        return remote(
+            self.source.at[jnp.clip(dest - self.at.core, 0, self.at.images - 1)],
+            self.target.at[:, self.columns()],
+            self.send.at[d],
+            self.recv.at[d],
+            (self.at.p, dest),
+        )
+
+    def own(self):
+        return pltpu.make_async_copy(
+            self.source.at[jnp.clip(self.at.slot, 0, self.at.images - 1)],
+            self.target.at[:, self.columns()],
+            self.local,
+        )
+
+    def start(self):
+        self.own().start()
+        for d in range(1, RING):
+            pl.when(self.at.holds(self.at.shifts[d]))(self.copy(d).start)
+
+    def here(self):
+        self.own().wait()
+        for d in range(1, RING):
+            pl.when(self.at.live)(self.copy(d).wait_recv)
+
+    def sent(self):
+        for d in range(1, RING):
+            pl.when(self.at.holds(self.at.shifts[d]))(self.copy(d).wait_send)
+
+
+def norm_rows(value, gain, shift):
+    middle = jnp.mean(value, 1, keepdims=True)
+    spread = jnp.mean(value * value, 1, keepdims=True) - middle * middle
+    return (value - middle) * lax.rsqrt(spread + EPS) * gain + shift
+
+
+def head_mask(lanes, h):
+    lane = lax.broadcasted_iota(jnp.int32, (1, lanes), 1)
+    return lax.rem(lane, 128) // 32 == h
+
+
+def forward_kernel(images, seq, *refs):
+    (
+        tokens,
+        cotangent,
+        small,
+        attn_in,
+        out_in,
+        fc1_in,
+        fc2_in,
+        dy_full,
+        small_full,
+        attn_full,
+        out_full,
+        fc1_full,
+        fc2_full,
+        x_rows_out,
+        h1_out,
+        qkv_out,
+        ctx_out,
+        r_out,
+        h2_out,
+        act_out,
+        slope_out,
+        x_full,
+        x_v,
+        h1_v,
+        h2_v,
+        qkv_v,
+        ctx_v,
+        r_v,
+        w_v,
+        act_v,
+        slope_v,
+        small_v,
+        bias_v,
+        row_send,
+        row_recv,
+        small_send,
+        small_recv,
+        z_send,
+        unit_send,
+        unit_recv,
+        local_sem,
+        w_sem,
+        tile_sem,
+        out_sem,
+    ) = refs
+    at = Place(images)
+    p, z = at.p, at.z
+    g = Gather(
+        at,
+        (attn_in, out_in, fc1_in, fc2_in),
+        (attn_full, out_full, fc1_full, fc2_full),
+        (z_send, unit_send, unit_recv),
+    )
+    x_rows = Rows(at, tokens, x_full, row_send.at[0], row_recv.at[0], local_sem.at[0])
+    dy_rows = Rows(at, cotangent, dy_full, row_send.at[1], row_recv.at[1], local_sem.at[1])
+    travel = x_full.shape[0]
+    full = x_full.shape[1]
+    quarter = full // RING
+
+    def small_copy(d):
+        return remote(
+            small, small_full.at[d], small_send.at[d], small_recv.at[d], (p, at.shifts[d])
+        )
+
+    small_own = pltpu.make_async_copy(small, small_full.at[0], local_sem.at[2])
+
+    at.greet()
+    g.z_start(0)
+    for d in range(1, RING):
+        small_copy(d).start()
+    small_own.start()
+    x_rows.start()
+    x_v[travel:] = jnp.zeros((ROWS - travel, full), x_v.dtype)
+
+    g.spread(0, 0)
+    g.spread(0, 1)
+    g.z_start(1)
+    g.spread(0, 2)
+    for d in range(1, RING):
+        small_copy(d).wait()
+    small_own.wait()
+    small_load = pltpu.make_async_copy(small_full, small_v, local_sem.at[3])
+    small_load.start()
+    x_rows.here()
+    x_load = pltpu.make_async_copy(x_full, x_v.at[pl.ds(0, travel)], local_sem.at[4])
+    x_load.start()
+    small_load.wait()
+
+    def feature(row, start):
+        parts = [
+            small_v[lax.rem(z + RING - j, RING), row : row + 1, start : start + quarter]
+            for j in range(RING)
+        ]
+        return wide(jnp.concatenate(parts, 1))
+
+    def unit_blocks(row, start, size):
+        return [
+            wide(small_v[k, row : row + 1, start : start + size]) for k in range(RING)
+        ]
+
+    gain, shift = feature(0, 0), feature(0, quarter)
+    for c, start in ((0, 2 * quarter), (2, 3 * quarter)):
+        for half in range(2):
+            blocks = unit_blocks(1, start + half * 128, 128)
+            bias_v[c : c + 1, half * TILE : (half + 1) * TILE] = jnp.concatenate(blocks, 1)
+    bias_v[1:2] = jnp.zeros((1, full), jnp.float32)
+    x_load.wait()
+
+    def first_norm(i, _):
+        block = rows_at(i * 16, 16)
+        value = jnp.where(at.live, wide(x_v[block]), 0.0)
+        x_v[block] = low(value)
+        h1_v[block] = low(norm_rows(value, gain, shift))
+        return 0
+
+    lax.fori_loop(0, ROWS // 16, first_norm, 0)
+    saves = [
+        pltpu.make_async_copy(x_v, x_rows_out, out_sem.at[0]),
+        pltpu.make_async_copy(h1_v, h1_out, out_sem.at[1]),
+    ]
+    for s in saves:
+        s.start()
+
+    for i in range(3):
+        g.relay(0, i)
+        g.spread(1, i)
+        if i == 1:
+            g.z_start(2)
+        if i:
+            g.share(0, i - 1)
+    g.share(0, 2)
+    g.whole(0)
+
+    def tile_load(chunk, c, slot):
+        return list(
+            weight_copies(
+                at,
+                (attn_in, out_in)[chunk],
+                (attn_full, out_full)[chunk],
+                chunk,
+                w_v.at[slot],
+                w_sem.at[slot],
+                c,
+            )
+        )
+
+    def go(copies):
+        for copy in copies:
+            copy.start()
+
+    def arrive(copies):
+        for copy in copies:
+            copy.wait()
+
+    def filled(slot):
+        pltpu.make_async_copy(w_v.at[slot], w_v.at[slot], w_sem.at[slot]).wait()
+
+    loads = [tile_load(0, c, c % 2) for c in range(3)] + [tile_load(1, 0, 1)]
+    go(loads[0])
+    go(loads[1])
+    steps = [
+        lambda: g.spread(2, 0),
+        lambda: g.relay(1, 0),
+        lambda: g.relay(1, 1),
+    ]
+    for c in range(3):
+        filled(c % 2)
+
+        def project(i, _, c=c):
+            block = rows_at(i * TILE, TILE)
+            out = dot_on(h1_v[...], w_v[c % 2, block], 1, 1)
+            lanes = pl.ds(pl.multiple_of(i * TILE, TILE), TILE)
+            qkv_v[c, :, lanes] = low(out + bias_v[c : c + 1, lanes])
+            return 0
+
+        lax.fori_loop(0, 2, project, 0)
+        if c == 0:
+            go(loads[2])
+        steps[c]()
+    save = pltpu.make_async_copy(qkv_v, qkv_out, out_sem.at[2])
+    save.start()
+    saves.append(save)
+
+    key = lax.broadcasted_iota(jnp.int32, (ROWS, 1), 0)
+
+    def attend(k, _):
+        lanes = [pl.ds(pl.multiple_of(k * 128 + half * TILE, 128), 128) for half in range(2)]
+
+        def group(c):
+            return jnp.concatenate([qkv_v[c, :, lane] for lane in lanes], 1)
+
+        keys, values = group(1), group(2)
+        for r in range(ROWS // 128):
+            block = slice(r * 128, (r + 1) * 128)
+            query = jnp.concatenate([qkv_v[0, block, lane] for lane in lanes], 1)
+            query = query * jnp.bfloat16(HD ** (-0.5))
+            out = None
+            for h in range(4):
+                mask = head_mask(256, h)
+                scores = dot_on(keys, jnp.where(mask, query, jnp.bfloat16(0)), 1, 1)
+                scores = jnp.where(key < seq, scores, -1e30)
+                expo = jnp.exp(scores - jnp.max(scores, 0, keepdims=True))
+                probs = low(expo * (1.0 / jnp.sum(expo, 0, keepdims=True)))
+                part = dot_on(probs, values, 0, 0)
+                out = part if out is None else jnp.where(mask, part, out)
+            out = low(out)
+            ctx_v[block, lanes[0]] = out[:, :128]
+            ctx_v[block, lanes[1]] = out[:, 128:]
+        return 0
+
+    attention_steps = [
+        [lambda: g.spread(2, 1), lambda: g.z_start(3), lambda: g.relay(1, 2)],
+        [lambda: g.spread(2, 2), lambda: g.share(1, 0), lambda: g.share(1, 1)],
+        [lambda: g.share(1, 2), lambda: g.relay(2, 0), lambda: g.spread(3, 0)],
+        [lambda: g.relay(2, 1), lambda: g.spread(3, 1), dy_rows.start],
+    ]
+    for k in range(4):
+        attend(k, 0)
+        for step in attention_steps[k]:
+            step()
+    g.whole(1)
+    go(loads[3])
+    save = pltpu.make_async_copy(ctx_v, ctx_out, out_sem.at[3])
+    save.start()
+    saves.append(save)
+    out_bias = feature(0, 2 * quarter)
+    gain2, shift2 = feature(0, 3 * quarter), feature(1, 0)
+    filled(1)
+    for i in range(2):
+        lanes = slice(i * TILE, (i + 1) * TILE)
+        attn = dot_on(ctx_v[...], w_v[1, :, lanes], 1, 0)
+        r_v[:, lanes] = wide(x_v[:, lanes]) + (attn + out_bias[:, lanes])
+    save = pltpu.make_async_copy(r_v, r_out, out_sem.at[4])
+    save.start()
+    saves.append(save)
+    g.relay(2, 2)
+    g.spread(3, 2)
+    g.share(2, 0)
+
+    def second_norm(i, _):
+        block = rows_at(i * 16, 16)
+        h2_v[block] = low(norm_rows(r_v[block], gain2, shift2))
+        return 0
+
+    lax.fori_loop(0, ROWS // 16, second_norm, 0)
+    save = pltpu.make_async_copy(h2_v, h2_out, out_sem.at[5])
+    save.start()
+    saves.append(save)
+    g.share(2, 1)
+    g.relay(3, 0)
+    g.share(2, 2)
+    g.whole(2)
+
+    def pair_load(i):
+        slot = i % 2
+        for side in range(2):
+            yield from weight_copies(
+                at,
+                fc1_in,
+                fc1_full,
+                2,
+                w_v.at[slot, pl.ds(side * TILE, TILE)],
+                w_sem.at[slot],
+                q=2 * i + side,
+            )
+
+    def tile_saves(q):
+        slot = q % 2
+        return [
+            pltpu.make_async_copy(act_v.at[slot], act_out.at[q], tile_sem.at[0, slot]),
+            pltpu.make_async_copy(slope_v.at[slot], slope_out.at[q], tile_sem.at[1, slot]),
+        ]
+
+    pairs = [list(pair_load(i)) for i in range(4)]
+    go(pairs[0])
+    go(pairs[1])
+    steps = [
+        [lambda: g.relay(3, 1)],
+        [lambda: g.relay(3, 2)],
+        [lambda: g.share(3, 0), lambda: g.share(3, 1)],
+        [lambda: g.share(3, 2)],
+    ]
+    for i in range(4):
+        filled(i % 2)
+        for side in range(2):
+            q = 2 * i + side
+            if q >= 2:
+                arrive(tile_saves(q - 2))
+            bias = jnp.concatenate(unit_blocks(2, q * 128, 128), 1)
+            for j in range(2):
+                cols = slice(j * 256, (j + 1) * 256)
+                start = side * TILE + j * 256
+                u = dot_on(h2_v[...], w_v[i % 2, start : start + 256], 1, 1) + bias[:, cols]
+                sg = 1.0 / (1.0 + jnp.exp(-1.702 * u))
+                act_v[side, :, cols] = low(u * sg)
+                slope_v[side, :, cols] = low(sg + 1.702 * u * sg * (1.0 - sg))
+            go(tile_saves(q))
+        if i < 2:
+            go(pairs[i + 2])
+        for step in steps[i]:
+            step()
+    for q in (6, 7):
+        arrive(tile_saves(q))
+    arrive(saves)
+    g.whole(3)
+    dy_rows.here()
+    for chunk in range(4):
+        g.sent(chunk)
+    x_rows.sent()
+    dy_rows.sent()
+
+
+def forward(seq, tokens, cotangent, small, attn_in, out_in, fc1_in, fc2_in):
+    images, rows, width = tokens.shape
+    full = RING * width
+    bf16 = jnp.bfloat16
+    f32 = jnp.float32
+    dma = pltpu.SemaphoreType.DMA
+    shapes = (
+        ((rows, full), bf16),
+        ((RING,) + small.shape, bf16),
+        ((3, 2, 384, full), bf16),
+        ((2, 384, full), bf16),
+        ((8, 384, full), bf16),
+        ((8, 384, full), bf16),
+        ((ROWS, full), bf16),
+        ((ROWS, full), bf16),
+        ((3, ROWS, full), bf16),
+        ((ROWS, full), bf16),
+        ((ROWS, full), f32),
+        ((ROWS, full), bf16),
+        ((8, ROWS, TILE), bf16),
+        ((8, ROWS, TILE), bf16),
+        ((rows, full), bf16),
+    )
+    return pl.pallas_call(
+        functools.partial(forward_kernel, images, seq),
+        out_shape=[jax.ShapeDtypeStruct(s, d) for s, d in shapes],
+        in_specs=[pl.BlockSpec(memory_space=pl.ANY)] * 7,
+        out_specs=[pl.BlockSpec(memory_space=pl.ANY)] * len(shapes),
+        scratch_shapes=[
+            pltpu.VMEM((ROWS, full), bf16),
+            pltpu.VMEM((ROWS, full), bf16),
+            pltpu.VMEM((ROWS, full), bf16),
+            pltpu.VMEM((3, ROWS, full), bf16),
+            pltpu.VMEM((ROWS, full), bf16),
+            pltpu.VMEM((ROWS, full), f32),
+            pltpu.VMEM((2, 1024, full), bf16),
+            pltpu.VMEM((2, ROWS, TILE), bf16),
+            pltpu.VMEM((2, ROWS, TILE), bf16),
+            pltpu.VMEM((RING,) + small.shape, bf16),
+            pltpu.VMEM((8, full), f32),
+            dma((2, RING)),
+            dma((2, RING)),
+            dma((RING,)),
+            dma((RING,)),
+            dma((4, RING, 2)),
+            dma((4, RING, 9)),
+            dma((4, RING, 9)),
+            dma((5,)),
+            dma((2,)),
+            dma((2, 2)),
+            dma((6,)),
+        ],
+        compiler_params=pltpu.CompilerParams(
+            collective_id=0, has_side_effects=True, vmem_limit_bytes=56 * 2**20
+        ),
+    )(tokens, cotangent, small, attn_in, out_in, fc1_in, fc2_in)
+
+
+class Reduce:
+    def __init__(self, place, sizes, outs, bufs, sems):
+        self.at = place
+        self.sizes = sizes
+        self.starts = [sum(sizes[:i]) for i in range(4)]
+        self.outs = outs
+        self.held, self.first, self.second, self.far, self.total, self.stage = bufs
+        self.core_send, self.core_recv, self.send, self.recv, self.local = sems
+
+    def rows(self, c):
+        return pl.ds(self.starts[c], self.sizes[c])
+
+    def give(self, group, xy, slot):
+        y, x = xy // 2, lax.rem(xy, 2)
+        c = min(group, 3)
+        if c < 2:
+            source, at = self.stage.at[slot], self.rows(c)
+        else:
+            source = self.stage.at[slot, :, pl.ds(xy * 32, 32)]
+            at = pl.ds(self.starts[c] + (group - c) * 32, 32)
+        return remote(
+            source,
+            self.held.at[y, x, :, at],
+            self.core_send.at[group, xy],
+            self.core_recv.at[group, xy],
+            self.at.near(1),
+        )
+
+    def hop(self, source, target, c, i, q):
+        return remote(source, target, self.send.at[c, i], self.recv.at[c, i], self.at.near(q))
+
+    def x_copy(self, c, y):
+        at = self.rows(c)
+        return self.hop(self.held.at[y, 1, 0:2, at], self.first.at[0, y, :, at], c, y, 2)
+
+    def y_copy(self, c, x):
+        at = self.rows(c)
+        return self.hop(self.held.at[1, x, 2:4, at], self.first.at[1, x, :, at], c, 2 + x, 4)
+
+    def xy_copy(self, c):
+        at = self.rows(c)
+        return self.hop(self.first.at[0, 1, :, at], self.second.at[0, :, at], c, 4, 4)
+
+    def yx_copy(self, c):
+        at = self.rows(c)
+        return self.hop(self.first.at[1, 1, :, at], self.second.at[1, :, at], c, 5, 2)
+
+    def z_copy(self, c, k):
+        return remote(
+            self.second.at[k // 2, k % 2, self.rows(c)],
+            self.far.at[k - 1, self.rows(c)],
+            self.send.at[c, 5 + k],
+            self.recv.at[c, 5 + k],
+            (self.at.p, self.at.shifts[RING - k]),
+        )
+
+    def out_copy(self, c, q):
+        return self.hop(self.total.at[self.rows(c)], self.outs[c].at[self.at.p], c, 8 + q, q)
+
+    def out_here(self, c, q):
+        block = self.outs[c].at[turned(self.at.p, q)]
+        self.hop(self.total.at[self.rows(c)], block, c, 8 + q, q).wait_recv()
+
+    def out_own(self, c):
+        return pltpu.make_async_copy(
+            self.total.at[self.rows(c)], self.outs[c].at[self.at.p], self.local.at[c]
+        )
+
+    def share(self, c, q):
+        block = self.outs[c].at[turned(self.at.p, q)]
+        return self.hop(block, block, c, 9 + q, 1)
+
+    def share_here(self, c, q):
+        block = self.outs[c].at[turned(self.at.p, q)]
+        theirs = self.outs[c].at[turned(self.at.p, q + 1)]
+        self.hop(block, theirs, c, 9 + q, 1).wait_recv()
+
+    def add(self, dest, *sources):
+        def body(i, _):
+            at = rows_at(i * 16, 16)
+            value = wide(sources[0][at])
+            for s in sources[1:]:
+                value = value + wide(s[at])
+            dest[at] = low(value)
+            return 0
+
+        lax.fori_loop(0, dest.shape[0] // 16, body, 0)
+
+    def turn(self, c):
+        at = self.rows(c)
+        self.x_copy(c, 1).wait_recv()
+        for k in range(2):
+            block = self.first.at[0, 1, k, at]
+            self.add(block, block, self.held.at[1, 0, k, at])
+        self.xy_copy(c).start()
+        self.y_copy(c, 1).wait_recv()
+        for k in range(2):
+            block = self.first.at[1, 1, k, at]
+            self.add(block, block, self.held.at[0, 1, 2 + k, at])
+        self.yx_copy(c).start()
+
+    def rise(self, c):
+        at = self.rows(c)
+        self.x_copy(c, 0).wait_recv()
+        self.xy_copy(c).wait_recv()
+        for k in range(2):
+            block = self.second.at[0, k, at]
+            self.add(block, block, self.first.at[0, 0, k, at], self.held.at[0, 0, k, at])
+        self.z_copy(c, 1).start()
+        self.y_copy(c, 0).wait_recv()
+        self.yx_copy(c).wait_recv()
+        for k in range(2):
+            block = self.second.at[1, k, at]
+            self.add(block, block, self.first.at[1, 0, k, at], self.held.at[0, 0, 2 + k, at])
+            self.z_copy(c, 2 + k).start()
+
+    def settle(self, c):
+        at = self.rows(c)
+        for k in range(1, RING):
+            self.z_copy(c, k).wait_recv()
+        self.add(
+            self.total.at[at], self.second.at[0, 0, at], *(self.far.at[k, at] for k in range(3))
+        )
+        self.out_own(c).start()
+        for q in (2, 4, 6, 1):
+            self.out_copy(c, q).start()
+
+    def spread(self, c):
+        for q in (2, 4, 6):
+            self.out_here(c, q)
+            self.share(c, q).start()
+
+    def finish(self, c):
+        self.out_here(c, 1)
+        for q in (2, 4, 6):
+            self.share_here(c, q)
+            self.share(c, q).wait_send()
+        for i in range(2):
+            self.x_copy(c, i).wait_send()
+            self.y_copy(c, i).wait_send()
+        self.xy_copy(c).wait_send()
+        self.yx_copy(c).wait_send()
+        for k in range(1, RING):
+            self.z_copy(c, k).wait_send()
+        for q in (2, 4, 6, 1):
+            self.out_copy(c, q).wait_send()
+        self.out_own(c).wait()
+
+
+class Return:
+    def __init__(self, place, source, target, send, recv):
+        self.at = place
+        self.source, self.target = source, target
+        self.send, self.recv = send, recv
+        self.rows, self.width = target.shape[1], target.shape[2]
+
+    def pair(self, plane):
+        columns = pl.ds(pl.multiple_of(plane * self.width, self.width), self.width)
+        slot = jnp.clip(self.at.slot, 0, self.at.images - 1)
+        return self.source.at[pl.ds(0, self.rows), columns], self.target.at[slot]
+
+    def copy(self, d):
+        source, target = self.pair(self.at.shifts[d])
+        return remote(
+            source, target, self.send.at[d], self.recv.at[d], (self.at.p, self.at.shifts[d])
+        )
+
+    def own(self):
+        return pltpu.make_async_copy(*self.pair(self.at.z), self.send.at[0])
+
+    def start(self):
+        pl.when(self.at.live)(self.own().start)
+        for d in range(1, RING):
+            pl.when(self.at.live)(self.copy(d).start)
+
+    def sent(self):
+        pl.when(self.at.live)(self.own().wait)
+        for d in range(1, RING):
+            pl.when(self.at.live)(self.copy(d).wait_send)
+
+    def here(self):
+        for d in range(1, RING):
+            other = lax.rem(self.at.z + RING - d, RING)
+            pl.when(self.at.holds(other))(self.copy(d).wait_recv)
+
+
+def norm_parts(value):
+    middle = jnp.mean(value, 1, keepdims=True)
+    spread = jnp.mean(value * value, 1, keepdims=True) - middle * middle
+    inverse = lax.rsqrt(spread + EPS)
+    return (value - middle) * inverse, inverse
+
+
+def norm_reverse(gradient, normalized, gain, inverse):
+    scaled = gradient * gain
+    first = jnp.mean(scaled, 1, keepdims=True)
+    second = jnp.mean(scaled * normalized, 1, keepdims=True)
+    return inverse * (scaled - first - normalized * second)
+
+
+def backward_kernel(images, seq, sizes, *refs):
+    (
+        mask_in,
+        small_full,
+        x_in,
+        h1_in,
+        qkv_in,
+        ctx_in,
+        r_in,
+        h2_in,
+        act_in,
+        slope_in,
+        dy_in,
+        attn_in,
+        out_in,
+        fc1_in,
+        fc2_in,
+        attn_full,
+        out_full,
+        fc1_full,
+        fc2_full,
+        block_out,
+        grad_out,
+        vector_out,
+        s2,
+        s1,
+        so,
+        sa,
+        held,
+        first,
+        second,
+        far,
+        total,
+        stage,
+        w_v,
+        dy_v,
+        h_v,
+        act_v,
+        du_v,
+        mlp_v,
+        dh_v,
+        r_v,
+        da_v,
+        ctx_v,
+        dctx_v,
+        qkv_v,
+        p_v,
+        ds_v,
+        dg_v,
+        blk_v,
+        sums_v,
+        dus_v,
+        small_v,
+        vec,
+        vec_far,
+        core_send,
+        core_recv,
+        send,
+        recv,
+        row_send,
+        row_recv,
+        vec_send,
+        vec_recv,
+        local_sem,
+        load_sem,
+        tile_sem,
+        w_sem,
+    ) = refs
+    at = Place(images)
+    p, z = at.p, at.z
+    full = x_in.shape[1]
+    quarter = full // RING
+    travel = dy_in.shape[0]
+    red = Reduce(
+        at,
+        sizes,
+        (s2, s1, so, sa),
+        (held, first, second, far, total, stage),
+        (core_send, core_recv, send, recv, local_sem),
+    )
+    blocks_back = Return(at, blk_v, block_out, row_send.at[0], row_recv.at[0])
+    grads_back = Return(at, blk_v, grad_out, row_send.at[1], row_recv.at[1])
+
+    def load(source, target, i):
+        return pltpu.make_async_copy(source, target, load_sem.at[i])
+
+    dy_load = load(dy_in, dy_v.at[pl.ds(0, travel)], 0)
+    h2_load = load(h2_in, h_v, 1)
+    r_load = load(r_in, r_v, 2)
+    ctx_load = load(ctx_in, ctx_v, 3)
+    qkv_load = load(qkv_in, qkv_v, 4)
+    small_load = load(small_full, small_v, 5)
+    h1_load = load(h1_in, h_v, 6)
+    x_load = load(x_in, dy_v, 7)
+
+    def tile_loads(q, slot):
+        yield pltpu.make_async_copy(act_in.at[q], act_v.at[slot], tile_sem.at[0, slot])
+        yield pltpu.make_async_copy(slope_in.at[q], du_v.at[slot], tile_sem.at[1, slot])
+        for side, (pieces, whole) in enumerate(((fc1_in, fc1_full), (fc2_in, fc2_full))):
+            yield from weight_copies(
+                at, pieces, whole, 2, w_v.at[slot, pl.ds(side * TILE, TILE)], w_sem.at[slot], q=q
+            )
+
+    def matrix_loads(chunk, c, slot):
+        pieces, whole = ((attn_in, attn_full), (out_in, out_full))[chunk]
+        return weight_copies(at, pieces, whole, chunk, w_v.at[slot], w_sem.at[slot], c)
+
+    def go(copies):
+        for copy in copies:
+            copy.start()
+
+    def filled(slot):
+        pltpu.make_async_copy(w_v.at[slot], w_v.at[slot], w_sem.at[slot]).wait()
+
+    def turn_of(i):
+        return jnp.where(i == 0, 3, jnp.where(i == 1, 1, jnp.where(i == 2, 2, 0)))
+
+    dy_load.start()
+    go(tile_loads(7, 0))
+    h2_load.start()
+    at.greet()
+    go(tile_loads(6, 1))
+    small_load.start()
+    r_load.start()
+    ctx_load.start()
+    qkv_load.start()
+
+    dy_v[travel:] = jnp.zeros((ROWS - travel, full), dy_v.dtype)
+    sums_v[...] = jnp.zeros_like(sums_v)
+    mask = mask_in[0:1, 0:1]
+    dy_load.wait()
+
+    def masked(i, _):
+        block = rows_at(i * 16, 16)
+        dy_v[block] = low(jnp.where(at.live, wide(dy_v[block]), 0.0) * mask)
+        return 0
+
+    lax.fori_loop(0, travel // 16, masked, 0)
+    h2_load.wait()
+
+    def halves(body):
+        lax.fori_loop(0, 2, lambda j, _: (body(pl.ds(pl.multiple_of(j * TILE, TILE), TILE)), 0)[1], 0)
+
+    def keep(group, xy, left, right):
+        y, x = xy // 2, lax.rem(xy, 2)
+        red.give(group, xy, 0).wait_recv()
+        at_rows = red.rows(group)
+
+        def body(cols):
+            grad = dot_on(left[...], right[:, cols], 0, 0)
+            for k in range(RING):
+                old = wide(held[y, x, k, at_rows, cols])
+                held[y, x, k, at_rows, cols] = low(old + grad[k * 128 : (k + 1) * 128])
+
+        halves(body)
+        pl.when(x == 1)(red.x_copy(group, y).start)
+        pl.when(y == 1)(red.y_copy(group, x).start)
+
+    def stage_fill(slot, left, right):
+        def body(cols):
+            grad = low(dot_on(left[...], right[:, cols], 0, 0))
+            for k in range(RING):
+                stage[slot, k, :, cols] = grad[k * 128 : (k + 1) * 128]
+
+        halves(body)
+
+    mlp_v[...] = jnp.zeros_like(mlp_v)
+    dh_v[...] = jnp.zeros_like(dh_v)
+
+    def hidden_tile(i, core):
+        slot = 1 - core
+        xy = turn_of(i)
+        q = 2 * xy + core
+        pltpu.make_async_copy(act_in.at[q], act_v.at[slot], tile_sem.at[0, slot]).wait()
+        if core:
+            pl.when(i > 0)(red.give(0, turn_of(i - 1), 0).wait_send)
+            stage_fill(0, act_v.at[slot], dy_v)
+            red.give(0, xy, 0).start()
+        else:
+            keep(0, xy, act_v.at[slot], dy_v)
+        pltpu.make_async_copy(slope_in.at[q], du_v.at[slot], tile_sem.at[1, slot]).wait()
+        filled(slot)
+
+        def slopes(j, _):
+            cols = pl.ds(pl.multiple_of(j * 256, 256), 256)
+            start = pl.ds(pl.multiple_of(TILE + j * 256, 256), 256)
+            dact = dot_on(dy_v[...], w_v[slot, start], 1, 1)
+            du = low(dact * wide(du_v[slot, :, cols]))
+            du_v[slot, :, cols] = du
+            dus_v[pl.ds(q, 1), cols] = jnp.sum(wide(du), 0, keepdims=True)
+            return 0
+
+        lax.fori_loop(0, 2, slopes, 0)
+        if core:
+            pl.when(i > 0)(red.give(1, turn_of(i - 1), 1).wait_send)
+            stage_fill(1, du_v.at[slot], h_v)
+            red.give(1, xy, 1).start()
+        else:
+            keep(1, xy, du_v.at[slot], h_v)
+
+        def back(cols):
+            mlp_v[:, cols] += dot_on(act_v[slot], w_v[slot, TILE:, cols], 1, 0)
+            dh_v[:, cols] += dot_on(du_v[slot], w_v[slot, :TILE, cols], 1, 0)
+
+        halves(back)
+
+        @pl.when(i < 3)
+        def _():
+            go(tile_loads(2 * turn_of(i + 1) + core, slot))
+
+    def hidden_tiles(i, _):
+        hidden_tile(i, 1)
+        hidden_tile(i, 0)
+        return 0
+
+    lax.fori_loop(0, 4, hidden_tiles, 0)
+    go(matrix_loads(1, 0, 0))
+    go(matrix_loads(0, 0, 1))
+    h1_load.start()
+
+    small_load.wait()
+
+    def feature(row, start):
+        parts = [
+            small_v[lax.rem(z + RING - j, RING), row : row + 1, start : start + quarter]
+            for j in range(RING)
+        ]
+        return wide(jnp.concatenate(parts, 1))
+
+    gain1, gain2 = feature(0, 0), feature(0, 3 * quarter)
+    fc2_bias = feature(1, quarter)
+    r_load.wait()
+
+    def collect(i, value):
+        sums_v[i] = sums_v[i] + (value[:8] + value[8:])
+
+    def second_norm(i, _):
+        block = rows_at(i * 16, 16)
+        r1 = r_v[block]
+        dy = wide(dy_v[block])
+        blk_v[block] = low((r1 + (mlp_v[block] + fc2_bias)) * mask)
+        hat, inverse = norm_parts(r1)
+        dh = dh_v[block]
+        dr1 = dy + norm_reverse(dh, hat, gain2, inverse)
+        da = low(dr1)
+        r_v[block] = dr1
+        da_v[block] = da
+        collect(2, wide(da))
+        collect(3, dh * hat)
+        collect(4, dh)
+        collect(5, dy)
+        return 0
+
+    lax.fori_loop(0, ROWS // 16, second_norm, 0)
+    blocks_back.start()
+    x_load.start()
+    ctx_load.wait()
+
+    pending = [[red.give(0, 0, 0)], [red.give(1, 0, 1)]]
+
+    def stage_free(slot):
+        for copy in pending[slot]:
+            copy.wait_send()
+        pending[slot] = []
+
+    def stage_go(slot, copies):
+        go(copies)
+        pending[slot] = copies
+
+    far_half = pl.ds(TILE, TILE)
+    near_half = pl.ds(0, TILE)
+    stage_free(0)
+    stage_fill(0, ctx_v.at[:, far_half], da_v)
+    stage_go(0, [red.give(2, xy, 0) for xy in range(4)])
+    filled(0)
+
+    def dctx_half(rows):
+        dctx_v[:, rows] = low(dot_on(da_v[...], w_v[0, rows], 1, 1))
+
+    halves(dctx_half)
+
+    def keep_heads(group, left, right):
+        c = min(group, 3)
+        start = red.starts[c] + (group - c) * 32
+        for xy in range(4):
+            red.give(group, xy, 0).wait_recv()
+        def body(cols):
+            grad = dot_on(left[...], right[:, cols], 0, 0)
+            for xy in range(4):
+                for k in range(RING):
+                    rows = slice(start, start + 32)
+                    at_row = k * 128 + xy * 32
+                    old = wide(held[xy // 2, xy % 2, k, rows, cols])
+                    held[xy // 2, xy % 2, k, rows, cols] = low(old + grad[at_row : at_row + 32])
+
+        halves(body)
+
+    def first_sends(c):
+        red.x_copy(c, 1).start()
+        red.y_copy(c, 1).start()
+        red.x_copy(c, 0).start()
+        red.y_copy(c, 0).start()
+
+    keep_heads(2, ctx_v.at[:, near_half], da_v)
+    first_sends(2)
+    go(matrix_loads(0, 1, 0))
+    qkv_load.wait()
+    red.turn(0)
+
+    key = lax.broadcasted_iota(jnp.int32, (ROWS, 1), 0)
+    scale = HD ** (-0.5)
+
+    def attend_back(k):
+        lanes = [pl.ds(pl.multiple_of(k * 128 + half * TILE, 128), 128) for half in range(2)]
+
+        def group(ref):
+            return jnp.concatenate([ref[:, lane] for lane in lanes], 1)
+
+        query = group(qkv_v.at[0]) * jnp.bfloat16(scale)
+        keys, values = group(qkv_v.at[1]), group(qkv_v.at[2])
+        dctx = group(dctx_v)
+        none = jnp.bfloat16(0)
+
+        def one_head(h, _):
+            mask = head_mask(256, h)
+            for r in range(ROWS // 128):
+                cols = slice(r * 128, (r + 1) * 128)
+                scores = dot_on(keys, jnp.where(mask, query[cols], none), 1, 1)
+                scores = jnp.where(key < seq, scores, -1e30)
+                expo = jnp.exp(scores - jnp.max(scores, 0, keepdims=True))
+                probs = expo * (1.0 / jnp.sum(expo, 0, keepdims=True))
+                dprobs = dot_on(values, jnp.where(mask, dctx[cols], none), 1, 1)
+                delta = jnp.sum(probs * dprobs, 0, keepdims=True)
+                p_v[:, cols] = low(probs)
+                ds_v[:, cols] = low(probs * (dprobs - delta))
+            dq = dot_on(ds_v[...], keys, 0, 0) * scale
+            dk = dot_on(ds_v[...], query, 1, 0)
+            dv = dot_on(p_v[...], dctx, 1, 0)
+            for c, value in enumerate((dq, dk, dv)):
+                dg_v[c] = jnp.where(mask, low(value), dg_v[c])
+            return 0
+
+        lax.fori_loop(0, 4, one_head, 0)
+        for c in range(3):
+            for half in range(2):
+                qkv_v[c, :, lanes[half]] = dg_v[c, :, half * 128 : (half + 1) * 128]
+
+    steps = [
+        [lambda: red.turn(1), lambda: red.turn(2)],
+        [lambda: red.rise(0)],
+        [lambda: red.rise(1)],
+        [lambda: red.rise(2), lambda: red.settle(0)],
+    ]
+    def attend_group(k, _):
+        attend_back(k)
+        for i in range(4):
+
+            @pl.when(k == i)
+            def _():
+                for step in steps[i]:
+                    step()
+
+        return 0
+
+    lax.fori_loop(0, 4, attend_group, 0)
+    h1_load.wait()
+    for c in range(3):
+        slot = (c + 1) % 2
+        stage_free(slot)
+        stage_fill(slot, qkv_v.at[c, :, far_half], h_v)
+        stage_go(slot, [red.give(3 + c, xy, slot) for xy in range(4)])
+    for c in range(3):
+        keep_heads(3 + c, qkv_v.at[c, :, near_half], h_v)
+    first_sends(3)
+    for c in range(3):
+        slot = (c + 1) % 2
+        filled(slot)
+
+        def spread_back(cols, c=c, slot=slot):
+            value = dot_on(qkv_v[c], w_v[slot, :, cols], 1, 0)
+            dh_v[:, cols] = value if c == 0 else value + dh_v[:, cols]
+
+        halves(spread_back)
+        if c == 0:
+            go(matrix_loads(0, 2, 1))
+    red.spread(0)
+    red.settle(1)
+    x_load.wait()
+    blocks_back.sent()
+
+    def first_norm(i, _):
+        block = rows_at(i * 16, 16)
+        hat, inverse = norm_parts(wide(dy_v[block]))
+        dh = dh_v[block]
+        blk_v[block] = low(r_v[block] + norm_reverse(dh, hat, gain1, inverse))
+        collect(0, dh * hat)
+        collect(1, dh)
+        return 0
+
+    lax.fori_loop(0, ROWS // 16, first_norm, 0)
+    grads_back.start()
+
+    for i in range(6):
+        value = jnp.sum(sums_v[i], 0, keepdims=True)
+        for j in range(RING):
+            for side in range(2):
+                start = j * quarter + side * 128
+                vec[j, 2 * i + side : 2 * i + side + 1] = value[:, start : start + 128]
+    lane = lax.broadcasted_iota(jnp.int32, (8, 128), 1)
+    for row, c in ((12, 0), (14, 2)):
+        value = jnp.sum(wide(qkv_v[c]), 0, keepdims=True)
+        for k in range(RING):
+            sides = [
+                jnp.broadcast_to(value[:, half * TILE + k * 128 : half * TILE + k * 128 + 128], (8, 128))
+                for half in range(2)
+            ]
+            odd = at.core == 1
+            sides = [jnp.where(odd, sides[1], sides[0]), jnp.where(odd, sides[0], sides[1])]
+            for half in range(2):
+                v = sides[half]
+                near = jnp.where(
+                    lax.rem(lane // 32, 2) == 0, pltpu.roll(v, 96, 1), pltpu.roll(v, 32, 1)
+                )
+                v = jnp.where(lax.rem(p // 2, 2) == 1, near, v)
+                v = jnp.where(p // 4 == 1, pltpu.roll(v, 64, 1), v)
+                vec[lax.rem(z + RING - k, RING), row + half : row + half + 1] = v[0:1]
+    for q in range(8):
+        for k in range(RING):
+            at_row = pl.ds(16 + turned(p, q), 1)
+            vec[lax.rem(z + RING - k, RING), at_row] = dus_v[q : q + 1, k * 128 : (k + 1) * 128]
+
+    def vec_copy(i):
+        return remote(vec, vec_far.at[i], vec_send.at[i], vec_recv.at[i], at.near((1, 2, 4)[i]))
+
+    def vec_z(d):
+        return remote(
+            vec.at[at.shifts[d]],
+            vec_far.at[3, d],
+            vec_send.at[2 + d],
+            vec_recv.at[2 + d],
+            (p, at.shifts[d]),
+        )
+
+    def vec_step(i):
+        vec_copy(i).wait()
+        vec[...] = vec[...] + vec_far[i]
+
+    vec_copy(0).start()
+    red.turn(3)
+    red.settle(2)
+    vec_step(0)
+    vec_copy(1).start()
+    red.spread(1)
+    vec_step(1)
+    vec_copy(2).start()
+    red.rise(3)
+    vec_step(2)
+    for d in range(1, RING):
+        vec_z(d).start()
+    red.spread(2)
+    red.settle(3)
+    for d in range(1, RING):
+        vec_z(d).wait()
+    vec[0] = vec[z] + (vec_far[3, 1] + (vec_far[3, 2] + vec_far[3, 3]))
+    vec_out = pltpu.make_async_copy(vec.at[0], vector_out, local_sem.at[4])
+    vec_out.start()
+    red.spread(3)
+    stage_free(0)
+    stage_free(1)
+    for c in range(4):
+        red.finish(c)
+    vec_out.wait()
+    blocks_back.here()
+    grads_back.sent()
+    grads_back.here()
+
+
+def backward(seq, images, mask, *arrays):
+    travel, full = arrays[9].shape
+    width = full // RING
+    bf16 = jnp.bfloat16
+    f32 = jnp.float32
+    dma = pltpu.SemaphoreType.DMA
+    attn_in, out_in, fc1_in, fc2_in = arrays[10:14]
+    sizes = (fc2_in.shape[1], fc1_in.shape[1], out_in.shape[1], 3 * attn_in.shape[2])
+    every = sum(sizes)
+    outs = [jax.ShapeDtypeStruct((images, travel, width), bf16)] * 2
+    outs.append(jax.ShapeDtypeStruct((24, 128), f32))
+    outs += [jax.ShapeDtypeStruct((8, n, full), bf16) for n in sizes]
+    any_space = pl.BlockSpec(memory_space=pl.ANY)
+    vm = pltpu.VMEM
+    return pl.pallas_call(
+        functools.partial(backward_kernel, images, seq, sizes),
+        out_shape=outs,
+        in_specs=[pl.BlockSpec(memory_space=vm)] + [any_space] * len(arrays),
+        out_specs=[any_space] * 7,
+        scratch_shapes=[
+            vm((2, 2, RING, every, full), bf16),
+            vm((2, 2, 2, every, full), bf16),
+            vm((2, 2, every, full), bf16),
+            vm((3, every, full), bf16),
+            vm((every, full), bf16),
+            vm((2, RING, 128, full), bf16),
+            vm((2, 1024, full), bf16),
+            vm((ROWS, full), bf16),
+            vm((ROWS, full), bf16),
+            vm((2, ROWS, TILE), bf16),
+            vm((2, ROWS, TILE), bf16),
+            vm((ROWS, full), f32),
+            vm((ROWS, full), f32),
+            vm((ROWS, full), f32),
+            vm((ROWS, full), bf16),
+            vm((ROWS, full), bf16),
+            vm((ROWS, full), bf16),
+            vm((3, ROWS, full), bf16),
+            vm((ROWS, ROWS), bf16),
+            vm((ROWS, ROWS), bf16),
+            vm((3, ROWS, 256), bf16),
+            vm((ROWS, full), bf16),
+            vm((6, 8, full), f32),
+            vm((8, TILE), f32),
+            vm(arrays[0].shape, bf16),
+            vm((RING, 24, 128), f32),
+            vm((4, RING, 24, 128), f32),
+            dma((6, RING)),
+            dma((6, RING)),
+            dma((4, 16)),
+            dma((4, 16)),
+            dma((2, RING)),
+            dma((2, RING)),
+            dma((6,)),
+            dma((6,)),
+            dma((5,)),
+            dma((8,)),
+            dma((2, 2)),
+            dma((2,)),
+        ],
+        compiler_params=pltpu.CompilerParams(
+            collective_id=1, has_side_effects=True, vmem_limit_bytes=60 * 2**20
+        ),
+    )(mask, *arrays)
+
+
+def pick(stack, index):
+    return lax.dynamic_index_in_dim(stack, index, 0, keepdims=False)
+
+
+def by_place(value, p):
+    return jnp.stack([pick(value, turned(p, q)) for q in range(8)])
+
+
+def prepare(tokens, cotangent, vectors, w_attn, qv_bias, w_out, w_fc1, b_fc1, w_fc2):
+    images, seq, width = tokens.shape
+    full = width * RING
+    p = lax.axis_index("dp")
+    attn = jnp.transpose(w_attn, (1, 2, 0)).reshape(3, 8, 32, full).transpose(1, 0, 2, 3)
+    out = w_out.reshape(8, 32, full)
+    fc1 = jnp.transpose(w_fc1).reshape(8, -1, full)
+    fc2 = w_fc2.reshape(8, -1, full)
+    qv = by_place(qv_bias.reshape(2, 8, 32).transpose(1, 0, 2), p)
+    qv = qv.reshape(4, 2, 2, 32).transpose(2, 1, 0, 3).reshape(-1)
+    hidden = by_place(b_fc1.reshape(8, -1), p).reshape(-1)
+    small = jnp.concatenate(list(vectors) + [qv, hidden]).reshape(3, full)
+    small = jnp.pad(small, ((0, 13), (0, 0)))
+    tail = ((0, 0), (0, -seq % 16), (0, 0))
+    return jnp.pad(tokens, tail), jnp.pad(cotangent, tail), small, attn, out, fc1, fc2
+
+
+def image_local(
+    tokens,
+    image_mask,
+    ln1_gain,
+    first_norm_bias,
+    w_attn,
+    qv_bias,
+    w_out,
+    b_out,
+    ln2_gain,
+    second_norm_bias,
+    w_fc1,
+    b_fc1,
+    w_fc2,
+    b_fc2,
+    cotangent,
+):
+    images, seq, width = tokens.shape
+    full = width * RING
+    p = lax.axis_index("dp")
+    slot = lax.axis_index("tensor") - p % 2
+    live = (slot >= 0) & (slot < images)
+    mask = jnp.where(live, pick(image_mask, jnp.clip(slot, 0, images - 1)), 0)
+    mask = jnp.full((8, 128), mask.astype(jnp.float32))
+    vectors = (ln1_gain, first_norm_bias, b_out, ln2_gain, second_norm_bias, b_fc2)
+    ready = prepare(tokens, cotangent, vectors, w_attn, qv_bias, w_out, w_fc1, b_fc1, w_fc2)
+    dy, small, *rest = forward(seq, *ready)
+    fulls, kept = rest[:4], rest[4:12]
+    block_out, input_grad, sums, s2, s1, so, sa = backward(
+        seq, images, mask, small, *kept, dy, *ready[3:], *fulls
+    )
+    pairs = sums.reshape(12, width)
+    grad_qv = pairs[6:8].reshape(2, 2, 4, 32).transpose(0, 2, 1, 3).reshape(2, width)
+    return (
+        block_out[:, :seq],
+        input_grad[:, :seq],
+        pairs[0],
+        pairs[1],
+        jnp.transpose(wide(sa).reshape(8, 3, 32, full), (3, 1, 0, 2)).reshape(full, 3, width),
+        grad_qv,
+        wide(so).reshape(width, full),
+        pairs[2],
+        pairs[3],
+        pairs[4],
+        jnp.transpose(wide(s1).reshape(-1, full)),
+        pairs[8:].reshape(-1),
+        wide(s2).reshape(-1, full),
+        pairs[5],
+    )
+
+
 def solution(mesh):
     in_specs = (
         P("dp", None, "tensor"),
@@ -269,4 +1722,13 @@
         P("tensor", None),
         P("tensor"),
     )
-    return jax.shard_map(local, mesh=mesh, in_specs=in_specs, out_specs=out_specs, check_vma=False)
+    owners = mesh.shape["dp"] == 8 and mesh.shape["tensor"] == RING
+
+    def block(*arrays):
+        images = arrays[0].shape[0] // mesh.shape["dp"]
+        body = image_local if owners and images < RING else local
+        return jax.shard_map(
+            body, mesh=mesh, in_specs=in_specs, out_specs=out_specs, check_vma=False
+        )(*arrays)
+
+    return block

time: 1180 us -> 402 us (0.34)
  waiting for transfers between devices: 825 us -> 0 us
  Pallas kernels: 0 us -> 351 us
  matrix products: 114 us -> 0 us
  blocking collectives: 98.8 us -> 0 us
  local copies, waits for them, and re-layouts: 75.8 us -> 35.9 us
  other arithmetic: 41.8 us -> 7.71 us
  between operations: 14.4 us -> 1.99 us
    reduce_scatter x4 -> x0, waiting for transfers between devices: 432 us -> none  [settle_sums(): return lax.psum_scatter(value, 'tensor', scatter_dimension=1, tiled=True)]
    pallas_call x0 -> x2, Pallas kernels: none -> 351 us  [the longest x1 200 us: backward(): pl.pallas_call(functools.partial(backward_kernel, images, seq, sizes), ou...]
    all_gather x4 -> x0, waiting for transfers between devices: 262 us -> none  [spread_features(): return lax.all_gather(value, 'tensor', axis=1, tiled=True)]
    psum x1 -> x0, waiting for transfers between devices: 131 us -> none  [local(): lax.psum((first_norm_gain_gradient, grad_ln1_bias, grad_w_attn, grad_qv_b...]
    dot_general x33 -> x0, matrix products: 114 us -> none  [the longest x3 20.1 us: back_dot(): lax.dot_general(left, right, (((1,), (1,)), ((), ())), preferred_element_...]
    psum x5 -> x0, blocking collectives: 98.8 us -> none  [the longest x2 38.6 us: norm_stats(): lax.psum((jnp.sum(value, 1), jnp.sum(value * value, 1)), 'tensor')]
    while x12 -> x0, local copies, waits for them, and re-layouts: 23.4 us -> none  [the longest x4 13.2 us: local(): context, log_total = lax.map(attend_image, (query, keys, values))]
    reduce_sum x10 -> x0, other arithmetic: 22.7 us -> none  [the longest x1 5.84 us: local(): grad_b_out = jnp.sum(dattn, 0, dtype=jnp.float32)]
  transfers between devices with their start and end apart: 9 -> 0, of which waited for: 9 -> 0; matrix products, arithmetic and copies ran while one was open for 5% -> 0% of each run, Pallas kernels for 0% -> 0%
where the time goes in v2:
time: 402 us; the launch traced here: 397 us
  Pallas kernels  351 us (87%)
  local copies, waits for them, and re-layouts  35.9 us (9%)
  other arithmetic  7.71 us (2%)
    pallas_call x1, Pallas kernels, backward(): pl.pallas_call(functools.partial(backward_kernel, images, seq, sizes), ou...  200 us
    pallas_call x1, Pallas kernels, forward(): pl.pallas_call(functools.partial(forward_kernel, images, seq), out_shape=...  151 us
    unnamed x24, local copies, waits for them, and re-layouts  8.51 us

profile of v2, /device:TPU:0, one launch (start us, length us, event | category | flops | bytes accessed | tf_op | source)
XLA Modules:
  0.0 396.5 jit_solution(8110136802404431940)
XLA Ops:
  0.6 0.0 copy-start.1
  0.7 0.0 copy-start
  0.8 1.4 dynamic_slice.54
  2.8 0.6 broadcast_in_dim.3.refs_0_
  3.4 0.8 reshape.118
  4.2 1.0 constant_dynamic-slice_fusion
  5.4 0.1 reshape.120
  5.5 0.8 dynamic-update-slice
  6.3 0.8 dynamic-update-slice.1
  7.1 0.8 dynamic-update-slice.2
  8.0 0.8 dynamic-update-slice.3
  8.8 0.8 dynamic-update-slice.4
  9.6 0.8 dynamic-update-slice.5
  10.5 0.2 dynamic-update-slice.6
  10.7 0.6 pad.13.refs_2_
  11.3 2.2 pad.11.refs_0_
  13.5 0.0 copy-done.1
  13.5 1.0 pad.12.refs_1_
  14.4 0.0 copy-done
  14.5 0.9 copy.50
  15.3 1.3 copy.91
  16.6 3.9 copy.52
  20.6 150.7 %shard_map.254 = (bf16[592,1024]{1,0:T(8,128)(2,1)}, bf16[4,16,1024]{2,1,0:T(8,128)(2,1)}, bf16[3,2,384,1024]{3,2,1,0:T(8,128)(2,1)}, bf16[2,384,1024]{2,1,0:T(8...) custom-call(bf16[3,592,256]{2,1,0:T(8,128)(2,1)} %pad.11.refs_0_, ...), custom_call_target="tpu_custom_call" | custom-call | tf_op jit(solution)/shard_map/pallas_call | solution.py:837
  171.3 200.2 %shard_map.255 = (bf16[3,592,256]{2,1,0:T(8,128)(2,1)}, bf16[3,592,256]{2,1,0:T(8,128)(2,1)}, f32[24,128]{1,0:T(8,128)}, bf16[8,128,1024]{2,1,0:T(8,128)(2,1)}, ...) custom-call(f32[8,128]{1,0:T(8,128)} %broadcast_in_dim.3.refs_0_, ...), custom_call_target="tpu_custom_call" | custom-call | tf_op jit(solution)/shard_map/pallas_call | solution.py:1563
  371.5 0.0 copy-start.2
  371.5 0.0 copy-start.3
  371.5 2.3 slice.38
  373.8 0.7 slice.42
  374.5 1.3 slice_bitcast_fusion
  375.7 1.4 slice_bitcast_fusion.1
  377.1 0.1 reshape.131
  377.2 0.7 reshape.132
  377.9 0.0 copy-done.2
  377.9 1.0 slice.39
  378.9 0.0 copy-done.3
  378.9 1.1 bitcast_convert_fusion.2
  380.0 1.8 copy.53
  381.8 2.4 copy.56
  384.2 6.6 %bitcast_convert_fusion = (f32[1024,1024]{1,0:T(8,128)}, f32[1024,1024]{1,0:T(8,128)}) fusion(bf16[8,128,1024]{2,1,0:T(8,128)(2,1)} %get-tuple-element.55, bf16[8,128,1024]{2,1,0:T(8,128)(2,1)} %get-tuple-element.54), kind=kLoop, calls=%fused_computation | loop fusion | flops 2097152 | bytes 12582912 | tf_op jit(solution)/shard_map/reshape | solution.py:1686
  390.8 5.3 %copy.55 = f32[1024,1024]{0,1:T(8,128)} copy(f32[1024,1024]{1,0:T(8,128)} %get-tuple-element.93) | data formatting | bytes 8388608 | tf_op jit(solution)/shard_map/transpose | solution.py:1684
  (15 shorter events, 0.2 us)
Async XLA Ops:
  0.6 12.8 %copy-start.1 = (bf16[3,577,256]{2,1,0:T(8,128)(2,1)S(1)}, bf16[3,577,256]{2,1,0:T(8,128)(2,1)}, u32[]{:S(2)}) copy-start(bf16[3,577,256]{2,1,0:T(8,128)(2,1)} %param.29) | copy-start | bytes 2658820
  0.7 13.8 %copy-start = (bf16[1024,3,256]{2,0,1:T(8,128)(2,1)S(1)}, bf16[1024,3,256]{2,0,1:T(8,128)(2,1)}, u32[]{:S(2)}) copy-start(bf16[1024,3,256]{2,0,1:T(8,128)(2,1)} %param.19) | copy-start | bytes 4718596
  371.5 6.4 %copy-start.2 = (bf16[3,592,256]{2,1,0:T(8,128)(2,1)S(1)}, bf16[3,592,256]{2,1,0:T(8,128)(2,1)}, u32[]{:S(2)}) copy-start(bf16[3,592,256]{2,1,0:T(8,128)(2,1)} %get-tuple-element.50) | copy-start | bytes 2727940
  371.5 7.4 %copy-start.3 = (bf16[8,32,1024]{2,1,0:T(8,128)(2,1)S(1)}, bf16[8,32,1024]{2,1,0:T(8,128)(2,1)}, u32[]{:S(2)}) copy-start(bf16[8,32,1024]{2,1,0:T(8,128)(2,1)} %get-tuple-element.53) | copy-start | bytes 1572868
